TPU v7x, 256 devices: a whole 4x4x8 slice. The times are simulated.
256 devices in a mesh: dp: 16 (over z_hi, y), tensor: 16 (over z_lo, x, core).
Axes of the slice: x: 4, y: 4, z: 8 (z_hi: 4, z_lo: 2; z = z_hi * 2 + z_lo), core: 2. Of those that a mesh axis runs over, the one named last changes fastest.
Arguments:
- layer_input: bfloat16 [16, 2, 256, 4096], P('dp', None, None, 'tensor'), may hold values from -6 to 6
- out_grad: bfloat16 [16, 2, 256, 4096], P('dp', None, None, 'tensor'), may hold values from -0.625 to 0.625
- norm_gain: float32 [4096], replicated, may hold values from 0.25 to 1.75
- gate_weight: bfloat16 [4096, 14336], P('dp', 'tensor'), may hold values from -0.09375 to 0.09375
- up_weight: bfloat16 [4096, 14336], P('dp', 'tensor'), may hold values from -0.09375 to 0.09375
- down_weight: bfloat16 [14336, 4096], P('tensor', 'dp'), may hold values from -0.046875 to 0.046875
- lengths: int32 [16, 2], P('dp'), may hold values from 1 to 256, as said below
- proj_in: bfloat16 [4096, 64], replicated, may hold values from -0.09375 to 0.09375
- proj_out: bfloat16 [14336, 64], P('tensor'), may hold values from -0.046875 to 0.046875
- queries: bfloat16 [4096, 4096], P('tensor', 'dp'), may hold values from -0.09375 to 0.09375
Outputs:
- grad_proj: float32 [16, 64, 64], P('dp')
- scores: float32 [16, 4096], P('dp', 'tensor')
Inputs may be any that keep to these rules, and one draw needn't show every extreme that they name: `lengths`: each side of a pair has between 1 and 256 valid tokens, always from position 0; the chosen side of the first pair is full.
All inputs are finite; a program needn't handle non-finite values.
Results may differ from a plain program's by a relative error of at most 0.006.
Values may be sent and summed in bfloat16 or wider, within the bound.
A program may use at most 128 MiB of HBM per device.

v0:
```python
import jax
import jax.numpy as jnp
from jax import lax
from jax.sharding import PartitionSpec as P


def on_device(
    layer_input,
    out_grad,
    norm_gain,
    gate_weight,
    up_weight,
    down_weight,
    lengths,
    proj_in,
    proj_out,
    queries,
):
    pairs = layer_input.shape[0]
    seq_len = layer_input.shape[2]
    inputs_all, grads_all = (
        lax.all_gather(layer_input, "tensor", axis=3, tiled=True),
        lax.all_gather(out_grad, "tensor", axis=3, tiled=True),
    )
    width = inputs_all.shape[3]
    values = inputs_all.reshape(-1, width).astype(jnp.float32)
    factor = lax.rsqrt(jnp.mean(values * values, axis=1, keepdims=True) + 1e-05)
    normed = (values * factor * norm_gain).astype(jnp.bfloat16)
    grads = grads_all.reshape(-1, width)
    columns = normed
    gate = jnp.dot(
        columns,
        lax.all_gather(gate_weight, "dp", axis=0, tiled=True),
        preferred_element_type=jnp.float32,
    )
    up = jnp.dot(
        columns,
        lax.all_gather(up_weight, "dp", axis=0, tiled=True),
        preferred_element_type=jnp.float32,
    )
    columns = grads
    back = lax.dot_general(
        columns,
        lax.all_gather(down_weight, "dp", axis=1, tiled=True),
        (((1,), (1,)), ((), ())),
        preferred_element_type=jnp.float32,
    )
    sig = jax.nn.sigmoid(gate)
    dgate = (back * up * sig * (1.0 + gate * (1.0 - sig))).astype(jnp.bfloat16)
    right = lax.psum(jnp.dot(dgate, proj_out, preferred_element_type=jnp.float32), "tensor")
    left = jnp.dot(normed, proj_in, preferred_element_type=jnp.float32)
    positions = jnp.arange(seq_len, dtype=jnp.int32)
    mask = (positions[None, None, :] < lengths[:, :, None]).astype(jnp.float32).reshape(pairs, -1)
    rank = left.shape[1]
    left_pairs = left.reshape(pairs, -1, rank) * mask[:, :, None]
    right_pairs = right.reshape(pairs, -1, rank)
    grad_proj = jnp.einsum("ptr,pts->prs", left_pairs, right_pairs, precision=lax.Precision.HIGHEST)
    flat = grad_proj.reshape(pairs, rank * rank).astype(jnp.bfloat16)
    columns = flat
    scores = lax.dot_general(
        columns,
        lax.all_gather(queries, "dp", axis=1, tiled=True),
        (((1,), (1,)), ((), ())),
        preferred_element_type=jnp.float32,
    )
    return (grad_proj, scores)


def solution(mesh):
    in_specs = (
        P("dp", None, None, "tensor"),
        P("dp", None, None, "tensor"),
        P(),
        P("dp", "tensor"),
        P("dp", "tensor"),
        P("tensor", "dp"),
        P("dp", None),
        P(),
        P("tensor", None),
        P("tensor", "dp"),
    )
    out_specs = (P("dp", None, None), P("dp", "tensor"))
    return jax.shard_map(
        on_device, mesh=mesh, in_specs=in_specs, out_specs=out_specs, check_vma=False
    )
```

profile of v0, /device:TPU:32, one launch (start us, length us, event | category | flops | bytes accessed | tf_op | source)
XLA Modules:
  0.0 647.1 jit_solution(11708064533031327551)
XLA Ops:
  7.2 0.7 all-gather.7.cloned.1.call-update
  8.0 0.7 all-gather.15.cloned.1.call-update
  8.7 0.7 all-gather.9.cloned.1.call-update
  9.5 0.5 all-gather.11.cloned.1.call-update
  10.0 0.5 all-gather.13.cloned.1.call-update
  10.6 49.4 %all-gather.7.cloned.1.call-done = bf16[1,2,256,4096]{3,2,1,0:T(8,128)(2,1)} async-done(((bf16[1,2,256,256]{3,2,1,0:T(8,128)(2,1)}), bf16[1,2,256,4096]{3,2,1,0:T(8,128)(2,1)}) %all-gather.7.cloned.1.call-update) | async-done | bytes 4194320 | tf_op jit(solution)/shard_map/all_gather | solution.py:22
  60.0 3.2 multiply_reduce_fusion
  63.3 0.2 copy-done.1
  63.5 3.7 fusion.1
  67.2 102.1 %all-gather.15.cloned.1.call-done = bf16[4096,896]{1,0:T(8,128)(2,1)} async-done(((bf16[256,896]{1,0:T(8,128)(2,1)}), bf16[4096,896]{1,0:T(8,128)(2,1)}) %all-gather.15.cloned.1.call-update) | async-done | bytes 7340048 | tf_op jit(solution)/shard_map/all_gather | solution.py:33
  169.2 10.1 %fusion.7 = f32[512,896]{1,0:T(8,128)} fusion(bf16[512,4096]{1,0:T(8,128)(2,1)} %fusion.1, bf16[4096,896]{1,0:T(8,128)(2,1)} %all-gather.15.cloned.1.call-done), kind=kOutput, calls=%fused_computation.14 | convolution fusion | flops 3758096384 | bytes 13369344 | tf_op jit(solution)/shard_map/dot_general | solution.py:31
  179.3 38.6 %all-gather.9.cloned.1.call-done = bf16[1,2,256,4096]{3,2,1,0:T(8,128)(2,1)} async-done(((bf16[1,2,256,256]{3,2,1,0:T(8,128)(2,1)}), bf16[1,2,256,4096]{3,2,1,0:T(8,128)(2,1)}) %all-gather.9.cloned.1.call-update) | async-done | bytes 4194320 | tf_op jit(solution)/shard_map/all_gather | solution.py:23
  217.9 113.1 %all-gather.11.cloned.1.call-done = bf16[896,4096]{1,0:T(8,128)(2,1)} async-done(((bf16[896,256]{1,0:T(8,128)(2,1)}), bf16[896,4096]{1,0:T(8,128)(2,1)}) %all-gather.11.cloned.1.call-update) | async-done | bytes 7340048 | tf_op jit(solution)/shard_map/all_gather | solution.py:44
  331.1 10.2 %fusion.6 = f32[512,896]{1,0:T(8,128)S(1)} fusion(bf16[512,4096]{1,0:T(8,128)(2,1)} %bitcast.35, bf16[896,4096]{1,0:T(8,128)(2,1)} %all-gather.11.cloned.1.call-done), kind=kOutput, calls=%fused_computation.13 | convolution fusion | flops 3758096384 | bytes 13369344 | tf_op jit(solution)/shard_map/dot_general | solution.py:42
  341.2 101.0 %all-gather.13.cloned.1.call-done = bf16[4096,896]{1,0:T(8,128)(2,1)} async-done(((bf16[256,896]{1,0:T(8,128)(2,1)}), bf16[4096,896]{1,0:T(8,128)(2,1)}) %all-gather.13.cloned.1.call-update) | async-done | bytes 7340048 | tf_op jit(solution)/shard_map/all_gather | solution.py:38
  442.3 10.4 %fusion.2 = f32[512,64]{1,0:T(8,128)} fusion(bf16[896,64]{0,1:T(8,128)(2,1)S(1)} %copy-done.4, f32[512,896]{1,0:T(8,128)} %fusion.7, f32[512,896]{1,0:T(8,128)S(1)} %fusion.6, bf16[512,4096]{1,0:T(8,128)(2,1)} %fusion.1, bf16[4096,896]{1,0:T(8,128)(2,1)} %all-gather.13.cloned.1.call-done), kind=kOutput, calls=%fused_computation.6 | convolution fusion | flops 3821404160 | bytes 15450112 | tf_op jit(solution)/shard_map/dot_general | solution.py:50
  452.7 0.7 all-gather.17.cloned.1.call-update
  453.5 0.1 lt.25
  453.5 3.4 convolution_multiply_fusion
  457.0 115.8 %all-reduce.2.cloned.1.call-done = f32[512,64]{1,0:T(8,128)} async-done(((f32[512,64]{1,0:T(8,128)}), f32[512,64]{1,0:T(8,128)}) %all-reduce.2.cloned.1.call-update) | async-done | bytes 131088 | tf_op jit(solution)/shard_map/psum | solution.py:50
  572.8 2.2 fusion.5
  574.9 0.1 reshape.73
  575.0 62.4 %all-gather.17.cloned.1.call-done = bf16[256,4096]{1,0:T(8,128)(2,1)} async-done(((bf16[256,256]{1,0:T(8,128)(2,1)}), bf16[256,4096]{1,0:T(8,128)(2,1)}) %all-gather.17.cloned.1.call-update) | async-done | bytes 2097168 | tf_op jit(solution)/shard_map/all_gather | solution.py:62
  637.4 2.8 fusion.8
  (22 shorter events, 0.3 us)
Async XLA Ops:
  7.2 446.4 %copy-start = (bf16[4096,64]{0,1:T(8,128)(2,1)S(1)}, bf16[4096,64]{0,1:T(8,128)(2,1)}, u32[]{:S(2)}) copy-start(bf16[4096,64]{0,1:T(8,128)(2,1)} %param.17) | copy-start | bytes 1572868
  7.2 56.1 %copy-start.2 = (f32[4096]{0:T(1024)S(1)}, f32[4096]{0:T(1024)}, u32[]{:S(2)}) copy-start(f32[4096]{0:T(1024)} %param.12) | copy-start | bytes 49156
  7.2 52.9 %all-gather.7.cloned.1.call-start = ((), (), s32[]{:S(2)}) async-start(), calls=%async_computation | async-start | bytes 4456448 | tf_op jit(solution)/shard_map/all_gather | solution.py:22
  7.9 161.3 %all-gather.15.cloned.1.call-start = ((), (), s32[]{:S(2)}) async-start(), calls=%async_computation.4 | async-start | bytes 7798784 | tf_op jit(solution)/shard_map/all_gather | solution.py:33
  8.7 209.2 %all-gather.9.cloned.1.call-start = ((), (), s32[]{:S(2)}) async-start(), calls=%async_computation.1 | async-start | bytes 4456448 | tf_op jit(solution)/shard_map/all_gather | solution.py:23
  9.4 321.6 %all-gather.11.cloned.1.call-start = ((), (), s32[]{:S(2)}) async-start(), calls=%async_computation.2 | async-start | bytes 7798784 | tf_op jit(solution)/shard_map/all_gather | solution.py:44
  10.0 432.3 %all-gather.13.cloned.1.call-start = ((), (), s32[]{:S(2)}) async-start(), calls=%async_computation.3 | async-start | bytes 7798784 | tf_op jit(solution)/shard_map/all_gather | solution.py:38
  10.6 562.2 %all-reduce.2.cloned.1.call-start = ((), (), s32[]{:S(2)}) async-start(), calls=%async_computation.5 | async-start | bytes 524288 | tf_op jit(solution)/shard_map/psum | solution.py:50
  60.0 3.4 copy-start.1
  331.1 111.2 %copy-start.4 = (bf16[896,64]{0,1:T(8,128)(2,1)S(1)}, bf16[896,64]{0,1:T(8,128)(2,1)}, u32[]{:S(2)}) copy-start(bf16[896,64]{0,1:T(8,128)(2,1)} %param.18) | copy-start | bytes 344068
  341.2 112.2 %copy-start.3 = (s32[1,2]{1,0:T(1,128)S(1)}, s32[1,2]{1,0:T(1,128)}, u32[]{:S(2)}) copy-start(s32[1,2]{1,0:T(1,128)} %param.16) | copy-start | bytes 28
  452.7 184.7 %all-gather.17.cloned.1.call-start = ((), (), s32[]{:S(2)}) async-start(), calls=%async_computation.6 | async-start | bytes 2228224 | tf_op jit(solution)/shard_map/all_gather | solution.py:62
Sparse Core Ops, SparseCore 0:
  9.8 50.2 all-gather.6
  62.5 106.7 all-gather.14
  171.0 46.8 all-gather.8
  220.2 110.8 all-gather.10
  333.3 108.8 all-gather.12
  452.8 119.9 all-reduce.1
  575.5 61.8 all-gather.16
where the time goes:
time: 651 us; the launch traced here: 647 us
  waiting for transfers between devices  586 us (90%)
  matrix products  39 us (6%)
  between operations  14.2 us (2%)
  other arithmetic  6.9 us (1%)
    psum x1, waiting for transfers between devices, on_device(): lax.psum(jnp.dot(dgate, proj_out, preferred_element_type=jnp.float32), 't...  116 us
    all_gather x1, waiting for transfers between devices, on_device(): lax.all_gather(down_weight, 'dp', axis=1, tiled=True)  113 us
    all_gather x1, waiting for transfers between devices, on_device(): lax.all_gather(gate_weight, 'dp', axis=0, tiled=True)  102 us
    all_gather x1, waiting for transfers between devices, on_device(): lax.all_gather(up_weight, 'dp', axis=0, tiled=True)  101 us
    all_gather x1, waiting for transfers between devices, on_device(): lax.all_gather(queries, 'dp', axis=1, tiled=True)  62.4 us
    all_gather x1, waiting for transfers between devices, on_device(): lax.all_gather(layer_input, 'tensor', axis=3, tiled=True)  49.4 us
    all_gather x1, waiting for transfers between devices, on_device(): lax.all_gather(out_grad, 'tensor', axis=3, tiled=True)  38.6 us
  transfers between devices with their start and end apart: 7, of which 7 were waited for; matrix products, arithmetic and copies ran while one was open for 5% of the time, Pallas kernels for 0%

commit v1 on v0

v1 whole, which is shorter than its diff:
```python
import jax
import jax.numpy as jnp
from jax import lax
from jax.experimental import pallas as pl
from jax.experimental.pallas import tpu as pltpu
from jax.sharding import PartitionSpec as P

MESH = pl.DeviceIdType.MESH
F32 = jnp.float32
BF16 = jnp.bfloat16
TOK = 512
KB = 256
NB = 16
HID = 896
RANK = 64


def mod(a, n):
    return lax.rem(a + 2 * n, n)


def coords():
    dp = lax.axis_index("dp")
    t = lax.axis_index("tensor")
    z_hi, y = dp // 4, lax.rem(dp, 4)
    z_lo, x, c = t // 8, lax.rem(t // 2, 4), lax.rem(t, 2)
    return x, y, 2 * z_hi + z_lo, c


def device(x, y, z, c):
    return ((z // 2) * 4 + y, lax.rem(z, 2) * 8 + x * 2 + c)


def gather_kernel(
    li, og, wg, wu, wd, po, pin, gain,
    out,
    tok, bwg, bwu, bwd, bpo, acc_g, acc_u, acc_b, acc_l, acc_s,
    r_tok, r_w, r_po, s_zw, s_zt, s_po, s_wz, s_wy, s_wc, s_tz, s_tx,
):
    x, y, z, c = coords()
    z_hi, z_lo = z // 2, lax.rem(z, 2)
    xp, xm, yp, ym = mod(x + 1, 4), mod(x - 1, 4), mod(y + 1, 4), mod(y - 1, 4)
    other = (x, y, z, 1 - c)
    ka, kc = lax.rem(z_hi, 2), z_hi // 2

    barrier = pltpu.get_barrier_semaphore()
    peers = [(xp, y, z, c), (xm, y, z, c), (x, yp, z, c), (x, ym, z, c), other]
    for dz in range(1, 8):
        for cc in (0, 1):
            peers.append((x, y, mod(z + dz, 8), cc))
    for p in peers:
        pl.semaphore_signal(barrier, inc=1, device_id=device(*p), device_id_type=MESH)
    pl.semaphore_wait(barrier, len(peers))

    waits = []

    def send(src, dst, ssem, rsem, to, cond=None):
        d = pltpu.make_async_remote_copy(
            src_ref=src, dst_ref=dst, send_sem=ssem, recv_sem=rsem,
            device_id=device(*to), device_id_type=MESH,
        )
        if cond is None:
            d.start()
            waits.append(d.wait_send)
        else:
            pl.when(cond)(lambda: d.start())
            waits.append(lambda: pl.when(cond)(lambda: d.wait_send()))

    halves = [(0, 0), (1, 0), (2, 0), (0, 1), (1, 1), (2, 1)]
    bufs = (bwg, bwu, bwd)

    def wslot(j, q):
        m, h = halves[q]
        n = KB // 2 if m < 2 else HID // 2
        return bufs[m].at[j, pl.ds(h * n, n)]

    def wsrc(q):
        m, h = halves[q]
        n = KB // 2 if m < 2 else HID // 2
        return (wg, wu, wd)[m].at[pl.ds(h * n, n)]

    def wwait(j, q):
        pltpu.make_async_copy(wslot(j, q), wslot(j, q), r_w.at[j, q]).wait()

    def twait(a, j):
        pltpu.make_async_copy(tok.at[a, j], tok.at[a, j], r_tok.at[a, j]).wait()

    kt = z_lo + 2 * c
    rel = mod(z_hi - kt, 4)
    f = lax.rem(z_hi, 2)
    jw = z_hi * 4 + y
    mine = rel == 0
    entry = jnp.where(rel == 1, 1, jnp.where(rel == 3, 0, 1 - z_lo))
    far_z = jnp.where(mine, mod(z + 1 - 2 * z_lo, 8), 2 * kt + entry)
    for q in range(6):
        send(wsrc(q), wslot(jw, q), s_zw.at[0, q], r_w.at[jw, q], (x, y, far_z, f))
    for q in range(6):
        send(wsrc(q), wslot(jw, q), s_zw.at[1, q], r_w.at[jw, q], other, mine & (f != c))

        def local(q=q):
            pltpu.make_async_copy(wsrc(q), wslot(jw, q), r_w.at[jw, q]).start()

        pl.when(mine & (f == c))(local)
    has_po = (z_lo == ka) & (c == kc)
    z1 = mod(z + 1 - 2 * z_lo, 8)
    send(po, bpo, s_po.at[0], r_po, other, has_po)
    send(po, bpo, s_po.at[1], r_po, (x, y, z1, 0), has_po)
    send(po, bpo, s_po.at[2], r_po, (x, y, z1, 1), has_po)
    pl.when(has_po)(lambda: pltpu.make_async_copy(po, bpo, r_po).start())

    b = lax.rem(z_hi, 2)
    i = z_hi // 2
    jt = z_lo * 8 + x * 2 + c
    aligned = z_lo == b
    step = jnp.where(aligned, 2, 1)
    for a in range(2):
        src = (li, og)[a]
        send(src, tok.at[a, jt], s_zt.at[0, a], r_tok.at[a, jt], (x, y, mod(z + step, 8), i))
        send(src, tok.at[a, jt], s_zt.at[1, a], r_tok.at[a, jt], (x, y, mod(z - step, 8), i))
        send(src, tok.at[a, jt], s_zt.at[2, a], r_tok.at[a, jt], other, aligned & (i != c))

        def local_t(src=src, a=a):
            pltpu.make_async_copy(src, tok.at[a, jt], r_tok.at[a, jt]).start()

        pl.when(aligned & (i == c))(local_t)

    s0 = lax.rem(c + z_hi, 2)
    zs = (mod(z_hi + s0, 4), mod(z_hi + s0 + 2, 4))

    def w_own(n):
        zz = zs[n]
        j = zz * 4 + y
        r = mod(zz - z_hi, 4)
        ent = jnp.where(r == 1, 1, jnp.where(r == 3, 0, 1 - ka))
        fwd = (r != 0) & (z_lo == ent)
        for q in range(6):
            wwait(j, q)
            send(wslot(j, q), wslot(j, q), s_wy.at[n, 0, q], r_w.at[j, q], (x, yp, z, c))
            send(wslot(j, q), wslot(j, q), s_wy.at[n, 1, q], r_w.at[j, q], (x, ym, z, c))
            send(wslot(j, q), wslot(j, q), s_wz.at[n, q], r_w.at[j, q], (x, y, z1, c), fwd)
            send(wslot(j, q), wslot(j, q), s_wc.at[n, 0, q], r_w.at[j, q], other)

    def w_next(n):
        zz = zs[n]
        jm, jp = zz * 4 + ym, zz * 4 + yp
        for q in range(6):
            for way, j, to in ((0, jm, yp), (1, jp, ym)):
                wwait(j, q)
                if q // 3 == way:
                    send(wslot(j, q), wslot(j, q), s_wy.at[n, way, 6 + q % 3], r_w.at[j, q], (x, to, z, c))
                send(wslot(j, q), wslot(j, q), s_wc.at[n, 1 + way, q], r_w.at[j, q], other)

    def w_last(n):
        j = zs[n] * 4 + mod(y + 2, 4)
        for q in range(6):
            wwait(j, q)
            send(wslot(j, q), wslot(j, q), s_wc.at[n, 3, q], r_w.at[j, q], other)

    r0 = mod(z - 2 * z_lo - 4 * c, 8)
    u0 = 1 - mod(r0 + 7, 8) // 4
    us = (u0, 1 - u0)

    def t_own(n):
        u = us[n]
        r = mod(r0 - u, 8)
        for cc in (0, 1):
            j = u * 8 + x * 2 + cc
            for a in (0, 1):
                twait(a, j)
                blk = tok.at[a, j]
                send(blk, blk, s_tx.at[n, cc, 0, a], r_tok.at[a, j], (xp, y, z, c))
                send(blk, blk, s_tx.at[n, cc, 1, a], r_tok.at[a, j], (xm, y, z, c))
                up = (r == 1) | (r == 2) if a == 0 else r == 1
                down = (r == 7) | (r == 6) if a == 1 else r == 7
                send(blk, blk, s_tz.at[n, cc, 0, a], r_tok.at[a, j], (x, y, mod(z + 2, 8), c), up)
                send(blk, blk, s_tz.at[n, cc, 1, a], r_tok.at[a, j], (x, y, mod(z - 2, 8), c), down)

    def t_next(n):
        u = us[n]
        for cc in (0, 1):
            jm, jp = u * 8 + xm * 2 + cc, u * 8 + xp * 2 + cc
            twait(0, jm)
            send(tok.at[0, jm], tok.at[0, jm], s_tx.at[n, cc, 0, 2], r_tok.at[0, jm], (xp, y, z, c))
            twait(1, jp)
            send(tok.at[1, jp], tok.at[1, jp], s_tx.at[n, cc, 1, 2], r_tok.at[1, jp], (xm, y, z, c))
            twait(1, jm)
            twait(0, jp)

    def t_last(n):
        for cc in (0, 1):
            j = us[n] * 8 + mod(x + 2, 4) * 2 + cc
            twait(0, j)
            twait(1, j)

    w_own(0)
    t_own(0)
    t_own(1)
    w_next(0)
    t_next(0)
    w_own(1)
    t_next(1)
    w_next(1)
    t_last(0)
    t_last(1)
    w_last(0)
    w_last(1)
    for n in range(2):
        zz = mod(zs[n] + 1, 4)
        for dy in range(4):
            j = zz * 4 + mod(y + dy, 4)
            for q in range(6):
                wwait(j, q)
    pltpu.make_async_copy(bpo, bpo, r_po).wait()
    for w in waits:
        w()

    for ref in (acc_g, acc_u, acc_b, acc_l, acc_s):
        ref[...] = jnp.zeros_like(ref)

    @pl.loop(0, NB)
    def _(j):
        v = tok[0, j].astype(F32)
        acc_s[...] += jnp.broadcast_to(jnp.sum(v * v, axis=1, keepdims=True), acc_s.shape)
        n = (v * gain[j]).astype(BF16)
        acc_g[...] += jnp.dot(n, bwg[j], preferred_element_type=F32)
        acc_u[...] += jnp.dot(n, bwu[j], preferred_element_type=F32)
        acc_l[...] += jnp.dot(n, pin[j], preferred_element_type=F32)
        acc_b[...] += lax.dot_general(
            tok[1, j], bwd[j], (((1,), (1,)), ((), ())), preferred_element_type=F32
        )

    out[...] = jnp.zeros_like(out)

    @pl.loop(0, TOK // 128)
    def _(t):
        rows = pl.ds(pl.multiple_of(t * 128, 128), 128)
        factor = lax.rsqrt(acc_s[rows, 0:1] * (1.0 / 4096.0) + 1e-05)
        gate = acc_g[rows, :] * factor
        up = acc_u[rows, :] * factor
        sig = 1.0 / (1.0 + jnp.exp(-gate))
        dgate = (acc_b[rows, :] * up * sig * (1.0 + gate * (1.0 - sig))).astype(BF16)
        right = jnp.dot(dgate, bpo[...], preferred_element_type=F32)
        left = acc_l[rows, :] * factor
        out[...] += lax.dot_general(
            left, right, (((0,), (0,)), ((), ())),
            precision=lax.Precision.HIGHEST, preferred_element_type=F32,
        )


def gathered(li, og, wg, wu, wd, po, pin, gain):
    any_ = pl.BlockSpec(memory_space=pl.ANY)
    vmem = pl.BlockSpec(memory_space=pltpu.VMEM)
    dma = pltpu.SemaphoreType.DMA
    return pl.pallas_call(
        gather_kernel,
        out_shape=jax.ShapeDtypeStruct((RANK, RANK), F32),
        in_specs=[any_] * 6 + [vmem] * 2,
        out_specs=vmem,
        scratch_shapes=[
            pltpu.VMEM((2, NB, TOK, KB), BF16),
            pltpu.VMEM((NB, KB, HID), BF16),
            pltpu.VMEM((NB, KB, HID), BF16),
            pltpu.VMEM((NB, HID, KB), BF16),
            pltpu.VMEM((HID, RANK), BF16),
            pltpu.VMEM((TOK, HID), F32),
            pltpu.VMEM((TOK, HID), F32),
            pltpu.VMEM((TOK, HID), F32),
            pltpu.VMEM((TOK, RANK), F32),
            pltpu.VMEM((TOK, 128), F32),
            dma((2, NB)),
            dma((NB, 6)),
            dma,
            dma((2, 6)),
            dma((3, 2)),
            dma((3,)),
            dma((2, 6)),
            dma((2, 2, 9)),
            dma((2, 4, 6)),
            dma((2, 2, 2, 2)),
            dma((2, 2, 2, 3)),
        ],
        compiler_params=pltpu.CompilerParams(
            collective_id=0, has_side_effects=True, vmem_limit_bytes=60 << 20
        ),
    )(li, og, wg, wu, wd, po, pin, gain)


def on_device(
    layer_input,
    out_grad,
    norm_gain,
    gate_weight,
    up_weight,
    down_weight,
    lengths,
    proj_in,
    proj_out,
    queries,
):
    seq = layer_input.shape[2]
    positions = jnp.arange(seq, dtype=jnp.int32)
    valid = positions[None, None, :] < lengths[:, :, None]
    grads = jnp.where(valid[..., None], out_grad, jnp.zeros_like(out_grad))
    part = gathered(
        layer_input.reshape(TOK, KB),
        grads.reshape(TOK, KB),
        gate_weight,
        up_weight,
        down_weight,
        proj_out,
        proj_in.reshape(NB, KB, RANK),
        norm_gain.reshape(NB, 1, KB),
    )
    _, y, z, c = coords()
    dp = lax.axis_index("dp")
    pair = (lax.rem(z, 2) + 2 * c) * 4 + y
    every = jnp.where(jnp.arange(16)[:, None, None] == pair, part[None], 0.0)
    every = lax.psum(every, ("dp", "tensor"))
    grad_proj = lax.dynamic_slice_in_dim(every, dp, 1, 0)
    flat = every.reshape(16, RANK * RANK).astype(BF16)
    block = lax.dynamic_slice_in_dim(flat, dp * KB, KB, 1)
    scores = lax.dot_general(
        block, queries, (((1,), (1,)), ((), ())), preferred_element_type=F32
    )
    scores = lax.psum_scatter(scores, "dp", scatter_dimension=0, tiled=True)
    return (grad_proj, scores)


def solution(mesh):
    in_specs = (
        P("dp", None, None, "tensor"),
        P("dp", None, None, "tensor"),
        P(),
        P("dp", "tensor"),
        P("dp", "tensor"),
        P("tensor", "dp"),
        P("dp", None),
        P(),
        P("tensor", None),
        P("tensor", "dp"),
    )
    out_specs = (P("dp", None, None), P("dp", "tensor"))
    return jax.shard_map(
        on_device, mesh=mesh, in_specs=in_specs, out_specs=out_specs, check_vma=False
    )
```

time: 651 us -> 539 us (0.83)
  waiting for transfers between devices: 586 us -> 262 us
  Pallas kernels: 0 us -> 168 us
  blocking collectives: 0 us -> 81.3 us
  matrix products: 39 us -> 0.15 us
  local copies, waits for them, and re-layouts: 0.38 us -> 8.92 us
    all_gather x6 -> x0, waiting for transfers between devices: 467 us -> none  [the longest x1 113 us: on_device(): lax.all_gather(down_weight, 'dp', axis=1, tiled=True)]
    pallas_call x0 -> x1, Pallas kernels: none -> 168 us  [gathered(): pl.pallas_call(gather_kernel, out_shape=jax.ShapeDtypeStruct((RANK, RANK)...]
    psum x1, waiting for transfers between devices: 116 us -> 262 us  [on_device(): every = lax.psum(every, ('dp', 'tensor'))]
    unnamed x0 -> x1, blocking collectives: none -> 81.3 us
    dot_general x6 -> x1, matrix products: 39 us -> 0.15 us  [on_device(): lax.dot_general(block, queries, (((1,), (1,)), ((), ())), preferred_eleme...]
    unnamed x13 -> x12, local copies, waits for them, and re-layouts: 0.22 us -> 7.28 us
  transfers between devices with their start and end apart: 7 -> 1, of which waited for: 7 -> 1; matrix products, arithmetic and copies ran while one was open for 5% -> 0% of each run, Pallas kernels for 0% -> 0%
where the time goes in v1:
time: 539 us; the launch traced here: 538 us
  waiting for transfers between devices  262 us (49%)
  Pallas kernels  168 us (31%)
  blocking collectives  81.3 us (15%)
  between operations  14.1 us (3%)
  local copies, waits for them, and re-layouts  8.92 us (2%)
    psum x1, waiting for transfers between devices, on_device(): every = lax.psum(every, ('dp', 'tensor'))  262 us
    pallas_call x1, Pallas kernels, gathered(): pl.pallas_call(gather_kernel, out_shape=jax.ShapeDtypeStruct((RANK, RANK)...  168 us
    unnamed x1, blocking collectives  81.3 us
  transfers between devices with their start and end apart: 1, of which 1 were waited for; matrix products, arithmetic and copies ran while one was open for 0% of the time, Pallas kernels for 0%

profile of v1, /device:TPU:32, one launch (start us, length us, event | category | flops | bytes accessed | tf_op | source)
XLA Modules:
  0.0 538.1 jit_solution(16458296279296978204)
XLA Ops:
  7.2 0.0 copy-start
  7.2 0.0 all-reduce.3.cloned.1.call-start
  7.3 0.0 copy-start.2
  7.3 0.6 copy-done.2
  7.9 0.1 iota_compare_fusion
  8.0 1.7 copy.15.po
  9.7 0.0 copy-start.1
  9.7 2.4 copy.14
  12.1 0.0 copy-done.1
  12.1 0.9 broadcast_select_fusion.1
  13.0 168.0 %shard_map.113 = f32[64,64]{1,0:T(8,128)} custom-call(bf16[512,256]{1,0:T(8,128)(2,1)} %bitcast.9, bf16[512,256]{1,0:T(8,128)(2,1)} %bitcast.8, bf16[256,896]{1,0:T(8,128)(2,1)} %wg.1, bf16[256,896]{1,0:T(8,128)(2,1)} %wu.1, bf16[896,256]{1,0:T(8,128)(2,1)} %wd.1, bf16[896,64]{1,0:T(8,128)(2,1)} %copy.15.po, bf16[16,256,64]{2,1,0:T(8,128)(2,1)} %bitcast.7, ...), custom_call_target="tpu_custom_call" | custom-call | tf_op jit(solution)/shard_map/pallas_call | solution.py:254
  181.0 1.6 broadcast_select_fusion
  182.6 0.0 all-reduce.3.cloned.1.call-update
  182.7 0.0 copy-start.3
  182.7 0.7 copy-done.3
  183.4 0.6 dynamic-slice
  183.9 261.9 %all-reduce.3.cloned.1.call-done = f32[16,64,64]{2,1,0:T(8,128)} async-done(((f32[16,64,64]{2,1,0:T(8,128)}), f32[16,64,64]{2,1,0:T(8,128)}) %all-reduce.3.cloned.1.call-update) | async-done | bytes 262160 | tf_op jit(solution)/shard_map/psum | solution.py:318
  445.9 1.1 convert_element_type.6
  446.9 0.3 convert_element_type.7
  447.2 0.0 copy-done
  447.2 0.2 fusion
  447.4 81.3 %all-reduce = f32[16,256]{1,0:T(8,128)S(1)} all-reduce(f32[16,256]{1,0:T(8,128)S(1)} %fusion), channel_id=2, replica_groups=mesh['dp'=16,'tensor'=16] {'dp'}, use_global_device_ids=true, to_apply=%region_1.2.clone | all-reduce | flops 4096 | bytes 32768
  528.6 1.2 constant_dynamic-slice_fusion
  529.9 1.4 constant_dynamic-slice_fusion.1
  (1 shorter events, 0.0 us)
Async XLA Ops:
  7.2 440.0 %copy-start = (bf16[256,256]{1,0:T(8,128)(2,1)S(1)}, bf16[256,256]{1,0:T(8,128)(2,1)}, u32[]{:S(2)}) copy-start(bf16[256,256]{1,0:T(8,128)(2,1)} %param.19) | copy-start | bytes 393220
  7.2 438.7 %all-reduce.3.cloned.1.call-start = ((), (), s32[]{:S(2)}) async-start(), calls=%async_computation | async-start | bytes 1048576 | tf_op jit(solution)/shard_map/psum | solution.py:318
  7.3 0.7 copy-start.2
  9.7 2.4 copy-start.1
  182.7 0.7 copy-start.3
Sparse Core Ops, SparseCore 0:
  182.8 263.0 all-reduce.2

commit v2 on v1

--- a/solution.py
+++ b/solution.py
@@ -34,7 +34,7 @@
 def gather_kernel(
     li, og, wg, wu, wd, po, pin, gain,
     out,
-    tok, bwg, bwu, bwd, bpo, acc_g, acc_u, acc_b, acc_l, acc_s,
+    tok, bwg, bwu, bwd, bpo, acc_g, acc_u, acc_b, acc_l, acc_s, acc_o,
     r_tok, r_w, r_po, s_zw, s_zt, s_po, s_wz, s_wy, s_wc, s_tz, s_tx,
 ):
     x, y, z, c = coords()
@@ -220,8 +220,15 @@
     @pl.loop(0, NB)
     def _(j):
         v = tok[0, j].astype(F32)
-        acc_s[...] += jnp.broadcast_to(jnp.sum(v * v, axis=1, keepdims=True), acc_s.shape)
-        n = (v * gain[j]).astype(BF16)
+        v = v * v
+        acc_s[...] += v[:, :128] + v[:, 128:]
+
+    mean = jnp.sum(acc_s[...], axis=1, keepdims=True) * (1.0 / 4096.0)
+    acc_s[...] = jnp.broadcast_to(lax.rsqrt(mean + 1e-05), acc_s.shape)
+
+    @pl.loop(0, NB)
+    def _(j):
+        n = (tok[0, j].astype(F32) * acc_s[:, 0:1] * gain[j]).astype(BF16)
         acc_g[...] += jnp.dot(n, bwg[j], preferred_element_type=F32)
         acc_u[...] += jnp.dot(n, bwu[j], preferred_element_type=F32)
         acc_l[...] += jnp.dot(n, pin[j], preferred_element_type=F32)
@@ -229,22 +236,125 @@
             tok[1, j], bwd[j], (((1,), (1,)), ((), ())), preferred_element_type=F32
         )
 
-    out[...] = jnp.zeros_like(out)
+    acc_o[...] = jnp.zeros_like(acc_o)
 
     @pl.loop(0, TOK // 128)
     def _(t):
         rows = pl.ds(pl.multiple_of(t * 128, 128), 128)
-        factor = lax.rsqrt(acc_s[rows, 0:1] * (1.0 / 4096.0) + 1e-05)
-        gate = acc_g[rows, :] * factor
-        up = acc_u[rows, :] * factor
+        gate = acc_g[rows, :]
         sig = 1.0 / (1.0 + jnp.exp(-gate))
-        dgate = (acc_b[rows, :] * up * sig * (1.0 + gate * (1.0 - sig))).astype(BF16)
+        dgate = (acc_b[rows, :] * acc_u[rows, :] * sig * (1.0 + gate * (1.0 - sig))).astype(BF16)
         right = jnp.dot(dgate, bpo[...], preferred_element_type=F32)
-        left = acc_l[rows, :] * factor
-        out[...] += lax.dot_general(
-            left, right, (((0,), (0,)), ((), ())),
+        acc_o[...] += lax.dot_general(
+            acc_l[rows, :], right, (((0,), (0,)), ((), ())),
             precision=lax.Precision.HIGHEST, preferred_element_type=F32,
         )
+
+    for j in range(NB):
+        out[j] = acc_o[4 * j:4 * j + 4, :]
+
+
+def finish_kernel(part, q, grad, score, got1, mine, got2, got3, got4, rows, r1, r2, r3, r4, s1, s2, s3, s4):
+    x, y, z, c = coords()
+    z_hi, z_lo = z // 2, lax.rem(z, 2)
+    ph = z_lo + 2 * c
+    piece = z_hi * 4 + x
+
+    def dev2(zh, yy, zl, xx, cc):
+        return (zh * 4 + yy, zl * 8 + xx * 2 + cc)
+
+    team = [(mod(z_hi + d // 4, 4), mod(x + d % 4, 4)) for d in range(1, 16)]
+    same_t = [(mod(z_hi + d // 4, 4), mod(y + d % 4, 4)) for d in range(1, 16)]
+    every_t = [(lax.rem(z_lo + d // 8, 2), mod(x + (d // 2) % 4, 4), lax.rem(c + d % 2, 2)) for d in range(16)]
+    barrier = pltpu.get_barrier_semaphore()
+
+    def tell(to):
+        pl.semaphore_signal(barrier, inc=1, device_id=to, device_id_type=MESH)
+
+    for zh, xx in team:
+        tell(dev2(zh, y, z_lo, xx, c))
+    for zh, yy in same_t:
+        tell(dev2(zh, yy, z_lo, x, c))
+    for d in range(16):
+        tell(dev2(d // 4, y, lax.rem(z_hi, 2), d % 4, z_hi // 2))
+        tell(dev2(z_hi, d // 4, d % 2, y, (d // 2) % 2))
+    pl.semaphore_wait(barrier, 62)
+    waits = []
+
+    def send(src, dst, ssem, rsem, to, self_=None):
+        d = pltpu.make_async_remote_copy(
+            src_ref=src, dst_ref=dst, send_sem=ssem, recv_sem=rsem, device_id=to, device_id_type=MESH,
+        )
+        if self_ is None:
+            d.start()
+            waits.append(d.wait_send)
+        else:
+            def stay():
+                pltpu.make_async_copy(src, dst, rsem).start()
+
+            pl.when(jnp.logical_not(self_))(lambda: d.start())
+            pl.when(self_)(stay)
+            waits.append(lambda: pl.when(jnp.logical_not(self_))(lambda: d.wait_send()))
+
+    def arrived(ref, sem):
+        pltpu.make_async_copy(ref, ref, sem).wait()
+
+    for n, (zh, xx) in enumerate(team):
+        send(part.at[zh * 4 + xx], got1.at[piece], s1.at[n], r1.at[piece], dev2(zh, y, z_lo, xx, c))
+    total = part[piece]
+    for zh, xx in team:
+        m = zh * 4 + xx
+        arrived(got1.at[m], r1.at[m])
+        total = total + got1[m]
+    mine[...] = total
+    pair = ph * 4 + y
+    for n, (zl, xx, cc) in enumerate(every_t):
+        send(mine, got3.at[pair], s3.at[n], r3.at[pair], dev2(z_hi, x, zl, xx, cc), (x == y) if n == 0 else None)
+    for n, (zl, xx, cc) in enumerate(every_t):
+        send(mine, got2.at[piece], s2.at[n], r2.at[piece], dev2(ph, y, zl, xx, cc), (ph == z_hi) if n == 0 else None)
+    for p in range(16):
+        arrived(got3.at[p], r3.at[p])
+    s = jnp.zeros((16, KB), F32)
+    for r in range(4):
+        f = got3[:, r, :].astype(BF16)
+        s = s + lax.dot_general(
+            f, q[:, r * RANK:(r + 1) * RANK], (((1,), (1,)), ((), ())), preferred_element_type=F32
+        )
+    for p in range(16):
+        rows[p] = s[p:p + 1, :]
+    me = z_hi * 4 + y
+    for n, (zh, yy) in enumerate(same_t):
+        send(rows.at[zh * 4 + yy], got4.at[me], s4.at[n], r4.at[me], dev2(zh, yy, z_lo, x, c))
+    for p in range(16):
+        arrived(got2.at[p], r2.at[p])
+        grad[p] = got2[p]
+    total = rows[me]
+    for zh, yy in same_t:
+        m = zh * 4 + yy
+        arrived(got4.at[m], r4.at[m])
+        total = total + got4[m]
+    score[...] = total
+    for w in waits:
+        w()
+
+
+def finish(part, queries):
+    vmem = pl.BlockSpec(memory_space=pltpu.VMEM)
+    dma = pltpu.SemaphoreType.DMA
+    piece = pltpu.VMEM((NB, 4, RANK), F32)
+    row = pltpu.VMEM((16, 1, KB), F32)
+    return pl.pallas_call(
+        finish_kernel,
+        out_shape=(
+            jax.ShapeDtypeStruct((NB, 4, RANK), F32),
+            jax.ShapeDtypeStruct((1, KB), F32),
+        ),
+        in_specs=[vmem] * 2,
+        out_specs=(vmem, vmem),
+        scratch_shapes=[piece, pltpu.VMEM((4, RANK), F32), piece, piece, row, row]
+        + [dma((16,))] * 8,
+        compiler_params=pltpu.CompilerParams(collective_id=1, has_side_effects=True),
+    )(part, queries)
 
 
 def gathered(li, og, wg, wu, wd, po, pin, gain):
@@ -253,7 +363,7 @@
     dma = pltpu.SemaphoreType.DMA
     return pl.pallas_call(
         gather_kernel,
-        out_shape=jax.ShapeDtypeStruct((RANK, RANK), F32),
+        out_shape=jax.ShapeDtypeStruct((NB, 4, RANK), F32),
         in_specs=[any_] * 6 + [vmem] * 2,
         out_specs=vmem,
         scratch_shapes=[
@@ -267,6 +377,7 @@
             pltpu.VMEM((TOK, HID), F32),
             pltpu.VMEM((TOK, RANK), F32),
             pltpu.VMEM((TOK, 128), F32),
+            pltpu.VMEM((RANK, RANK), F32),
             dma((2, NB)),
             dma((NB, 6)),
             dma,
@@ -311,19 +422,8 @@
         proj_in.reshape(NB, KB, RANK),
         norm_gain.reshape(NB, 1, KB),
     )
-    _, y, z, c = coords()
-    dp = lax.axis_index("dp")
-    pair = (lax.rem(z, 2) + 2 * c) * 4 + y
-    every = jnp.where(jnp.arange(16)[:, None, None] == pair, part[None], 0.0)
-    every = lax.psum(every, ("dp", "tensor"))
-    grad_proj = lax.dynamic_slice_in_dim(every, dp, 1, 0)
-    flat = every.reshape(16, RANK * RANK).astype(BF16)
-    block = lax.dynamic_slice_in_dim(flat, dp * KB, KB, 1)
-    scores = lax.dot_general(
-        block, queries, (((1,), (1,)), ((), ())), preferred_element_type=F32
-    )
-    scores = lax.psum_scatter(scores, "dp", scatter_dimension=0, tiled=True)
-    return (grad_proj, scores)
+    grad, scores = finish(part, queries)
+    return (grad.reshape(1, RANK, RANK), scores)
 
 
 def solution(mesh):

time: 539 us -> 221 us (0.41)
  waiting for transfers between devices: 262 us -> 0 us
  blocking collectives: 81.3 us -> 0 us
  Pallas kernels: 168 us -> 210 us
  between operations: 14.1 us -> 0.67 us
    psum x1 -> x0, waiting for transfers between devices: 262 us -> none  [on_device(): every = lax.psum(every, ('dp', 'tensor'))]
    unnamed x1 -> x0, blocking collectives: 81.3 us -> none
    pallas_call x1 -> x2, Pallas kernels: 168 us -> 210 us  [the longest x1 169 us: gathered(): pl.pallas_call(gather_kernel, out_shape=jax.ShapeDtypeStruct((NB, 4, RANK...]
  transfers between devices with their start and end apart: 1 -> 0, of which waited for: 1 -> 0; matrix products, arithmetic and copies ran while one was open for 0% -> 0% of each run, Pallas kernels for 0% -> 0%
where the time goes in v2:
time: 221 us; the launch traced here: 219 us
  Pallas kernels  210 us (95%)
  local copies, waits for them, and re-layouts  5.01 us (2%)
  other arithmetic  2.58 us (1%)
    pallas_call x1, Pallas kernels, gathered(): pl.pallas_call(gather_kernel, out_shape=jax.ShapeDtypeStruct((NB, 4, RANK...  169 us
    pallas_call x1, Pallas kernels, finish(): pl.pallas_call(finish_kernel, out_shape=(jax.ShapeDtypeStruct((NB, 4, RAN...  41.2 us
    unnamed x8, local copies, waits for them, and re-layouts  5.01 us

profile of v2, /device:TPU:32, one launch (start us, length us, event | category | flops | bytes accessed | tf_op | source)
XLA Modules:
  0.0 218.7 jit_solution(12275369648568914578)
XLA Ops:
  0.6 0.0 copy-start
  0.6 0.8 iota_compare_fusion
  1.4 1.7 copy.13.po
  3.2 1.8 broadcast_select_fusion
  5.0 0.0 copy-done
  5.0 1.3 copy.12
  6.3 169.2 %shard_map.113.part = f32[16,4,64]{2,1,0:T(4,128)} custom-call(bf16[512,256]{1,0:T(8,128)(2,1)} %bitcast.8, bf16[512,256]{1,0:T(8,128)(2,1)} %bitcast.7, bf16[256,896]{1,0:T(8,128)(2,1)} %wg.1, bf16[256,896]{1,0:T(8,128)(2,1)} %wu.1, bf16[896,256]{1,0:T(8,128)(2,1)} %wd.1, bf16[896,64]{1,0:T(8,128)(2,1)} %copy.13.po, bf16[16,256,64]{2,1,0:T(8,128)(2,1)} %bitcast.6, ...), custom_call_target="tpu_custom_call" | custom-call | tf_op jit(solution)/shard_map/pallas_call | solution.py:364
  175.5 41.2 %shard_map.114 = (f32[16,4,64]{2,1,0:T(4,128)}, f32[1,256]{1,0:T(1,128)}) custom-call(f32[16,4,64]{2,1,0:T(4,128)} %shard_map.113.part, bf16[256,256]{1,0:T(8,128)(2,1)} %q.1), custom_call_target="tpu_custom_call" | custom-call | tf_op jit(solution)/shard_map/pallas_call | solution.py:346
  216.7 0.0 copy-start.1
  216.7 1.4 copy.16
  218.1 0.0 copy-done.1
  218.1 0.6 copy.17
Async XLA Ops:
  0.6 4.3 %copy-start = (bf16[4096,64]{0,1:T(8,128)(2,1)S(1)}, bf16[4096,64]{0,1:T(8,128)(2,1)}, u32[]{:S(2)}) copy-start(bf16[4096,64]{0,1:T(8,128)(2,1)} %param.17) | copy-start | bytes 1572868
  216.7 1.4 copy-start.1

commit v3 on v2

v3 whole, which is shorter than its diff:
```python
import jax
import jax.numpy as jnp
from jax import lax
from jax.experimental import pallas as pl
from jax.experimental.pallas import tpu as pltpu
from jax.sharding import PartitionSpec as P

MESH = pl.DeviceIdType.MESH
F32 = jnp.float32
BF16 = jnp.bfloat16
TOK = 512
KB = 256
NB = 16
HID = 896
RANK = 64
NSEND = 176

ORDERS = (
    (
        0, 1, 2, 3, 4, 5, 8, 9, 10, 11, 12, 13, 28, 29, 30, 31, 6, 7, 22, 20, 23, 21, 32, 33,
        54, 24, 52, 34, 35, 55, 25, 53, 36, 37, 14, 38, 39, 56, 73, 57, 15, 60, 63, 72, 74, 61, 64, 41,
        62, 16, 26, 40, 65, 42, 43, 27, 58, 44, 45, 59, 17, 66, 75, 18, 47, 67, 49, 68, 69, 46, 19, 70,
        48, 51, 50, 71,
    ),
    (
        0, 1, 2, 3, 4, 5, 8, 6, 7, 9, 28, 29, 10, 30, 31, 11, 33, 60, 12, 32, 35, 37, 61, 13,
        34, 63, 14, 20, 27, 36, 64, 52, 24, 59, 39, 62, 38, 41, 21, 15, 65, 56, 40, 43, 16, 53, 42, 72,
        17, 45, 66, 47, 44, 18, 22, 25, 67, 69, 54, 19, 57, 23, 46, 49, 74, 26, 68, 51, 55, 48, 58, 70,
        50, 73, 75, 71,
    ),
    (
        0, 1, 2, 3, 4, 5, 8, 6, 7, 14, 28, 29, 9, 41, 15, 40, 22, 31, 26, 60, 10, 43, 54, 16,
        30, 33, 58, 23, 42, 27, 45, 11, 17, 66, 55, 35, 32, 59, 18, 12, 47, 44, 73, 20, 63, 19, 21, 61,
        75, 52, 13, 49, 67, 37, 53, 34, 24, 69, 72, 46, 56, 25, 51, 62, 39, 48, 57, 70, 36, 74, 64, 68,
        71, 50, 65, 38,
    ),
    (
        0, 1, 2, 3, 4, 5, 8, 6, 7, 28, 29, 9, 14, 60, 31, 22, 30, 10, 41, 54, 40, 33, 23, 11,
        61, 35, 32, 55, 12, 63, 66, 26, 13, 73, 37, 34, 58, 15, 39, 62, 27, 64, 36, 16, 59, 43, 38, 24,
        65, 20, 75, 42, 17, 45, 56, 44, 47, 25, 52, 67, 18, 21, 19, 69, 46, 57, 53, 49, 68, 74, 72, 51,
        48, 70, 50, 71,
    ),
    (
        0, 1, 2, 3, 4, 5, 8, 6, 7, 9, 28, 29, 22, 30, 31, 10, 54, 60, 33, 23, 61, 11, 26, 55,
        35, 32, 34, 63, 58, 12, 73, 27, 13, 62, 37, 20, 36, 59, 39, 21, 52, 38, 64, 14, 75, 65, 40, 53,
        41, 66, 24, 72, 15, 16, 56, 17, 42, 43, 25, 18, 19, 44, 45, 57, 47, 46, 49, 67, 51, 74, 48, 69,
        50, 70, 68, 71,
    ),
    (
        0, 1, 2, 3, 4, 5, 8, 6, 7, 14, 28, 29, 9, 15, 40, 41, 31, 22, 60, 10, 43, 16, 54, 30,
        33, 45, 42, 23, 11, 17, 66, 35, 55, 12, 26, 32, 47, 73, 18, 44, 13, 63, 58, 27, 61, 37, 67, 19,
        59, 69, 24, 20, 34, 49, 75, 46, 56, 39, 25, 21, 36, 52, 64, 62, 51, 48, 70, 57, 68, 53, 65, 38,
        74, 71, 50, 72,
    ),
    (
        0, 1, 2, 3, 4, 5, 8, 6, 7, 20, 21, 22, 23, 9, 14, 52, 28, 29, 53, 10, 24, 40, 41, 54,
        55, 11, 30, 31, 25, 72, 56, 12, 33, 60, 15, 73, 57, 32, 35, 13, 74, 37, 66, 26, 34, 43, 16, 61,
        63, 27, 58, 36, 39, 42, 64, 59, 45, 62, 17, 75, 38, 65, 44, 47, 67, 69, 18, 46, 19, 49, 68, 51,
        48, 70, 50, 71,
    ),
    (
        0, 1, 2, 3, 4, 5, 8, 9, 10, 11, 12, 13, 28, 29, 30, 31, 6, 7, 32, 33, 34, 35, 36, 37,
        38, 39, 60, 63, 61, 64, 26, 20, 62, 65, 58, 52, 14, 15, 21, 40, 41, 53, 16, 42, 43, 72, 17, 45,
        66, 18, 47, 44, 25, 19, 49, 57, 67, 24, 69, 22, 56, 46, 51, 54, 23, 74, 48, 70, 27, 55, 68, 59,
        71, 50, 73, 75,
    ),
    (
        0, 1, 2, 3, 4, 5, 8, 9, 10, 11, 12, 13, 28, 29, 30, 31, 6, 7, 32, 33, 34, 35, 36, 37,
        38, 39, 60, 63, 61, 64, 22, 62, 65, 25, 54, 14, 57, 23, 15, 40, 41, 16, 43, 55, 42, 73, 17, 45,
        66, 26, 18, 47, 58, 44, 19, 49, 67, 20, 69, 46, 21, 52, 51, 27, 24, 53, 48, 59, 70, 68, 50, 71,
        56, 72, 75, 74,
    ),
    (
        0, 1, 2, 3, 4, 5, 8, 6, 7, 22, 23, 20, 21, 9, 14, 54, 28, 29, 55, 10, 26, 40, 41, 52,
        53, 11, 30, 31, 27, 73, 58, 12, 33, 60, 15, 72, 59, 32, 35, 13, 75, 37, 66, 24, 34, 43, 16, 61,
        63, 25, 36, 39, 56, 42, 64, 57, 45, 62, 38, 65, 17, 74, 44, 18, 47, 67, 49, 46, 69, 19, 68, 70,
        48, 51, 50, 71,
    ),
    (
        0, 1, 2, 3, 4, 5, 8, 6, 7, 14, 28, 29, 9, 15, 40, 41, 31, 20, 60, 10, 43, 16, 52, 30,
        33, 45, 42, 21, 11, 17, 66, 35, 53, 12, 32, 24, 72, 47, 18, 44, 13, 56, 63, 25, 61, 37, 67, 19,
        57, 69, 26, 22, 34, 74, 49, 46, 58, 39, 36, 27, 23, 64, 54, 62, 51, 48, 70, 59, 68, 65, 55, 38,
        71, 75, 50, 73,
    ),
    (
        0, 1, 2, 3, 4, 5, 8, 6, 7, 9, 28, 29, 20, 30, 31, 10, 52, 60, 33, 21, 61, 11, 24, 53,
        35, 32, 12, 34, 63, 56, 72, 25, 13, 62, 37, 22, 36, 57, 39, 23, 54, 38, 64, 14, 74, 65, 40, 55,
        41, 66, 26, 73, 15, 58, 16, 17, 42, 43, 27, 18, 19, 44, 45, 59, 47, 46, 49, 67, 51, 75, 48, 69,
        50, 70, 68, 71,
    ),
    (
        0, 1, 2, 3, 4, 5, 8, 6, 7, 28, 29, 9, 14, 60, 31, 20, 30, 10, 41, 52, 40, 33, 21, 61,
        11, 35, 32, 53, 12, 66, 63, 24, 13, 72, 34, 37, 56, 15, 62, 39, 25, 36, 64, 16, 57, 38, 43, 26,
        22, 74, 42, 65, 17, 58, 44, 45, 27, 54, 67, 18, 23, 47, 19, 46, 59, 49, 55, 68, 69, 75, 73, 48,
        51, 70, 50, 71,
    ),
    (
        0, 1, 2, 3, 4, 5, 8, 6, 7, 14, 28, 29, 9, 41, 15, 40, 20, 31, 24, 60, 10, 43, 52, 16,
        30, 33, 56, 21, 42, 25, 45, 11, 17, 66, 53, 35, 32, 57, 18, 12, 47, 44, 72, 22, 63, 19, 23, 61,
        74, 54, 13, 49, 67, 69, 55, 34, 26, 37, 73, 46, 58, 27, 51, 62, 70, 48, 59, 39, 36, 75, 64, 68,
        71, 50, 65, 38,
    ),
    (
        0, 1, 2, 3, 4, 5, 8, 6, 7, 9, 28, 29, 10, 30, 31, 11, 33, 60, 12, 32, 35, 37, 61, 13,
        34, 63, 22, 14, 24, 36, 64, 54, 56, 39, 62, 23, 38, 41, 15, 27, 65, 55, 40, 43, 16, 59, 42, 73,
        45, 66, 26, 17, 58, 44, 18, 47, 20, 75, 67, 52, 19, 49, 46, 21, 69, 25, 53, 68, 51, 48, 57, 50,
        70, 72, 71, 74,
    ),
    (
        0, 1, 2, 3, 4, 5, 8, 9, 10, 11, 12, 13, 28, 29, 30, 31, 6, 7, 20, 22, 21, 23, 32, 33,
        52, 26, 54, 34, 35, 53, 27, 55, 36, 37, 14, 38, 39, 58, 72, 59, 15, 60, 63, 73, 75, 61, 64, 41,
        62, 24, 40, 65, 16, 25, 42, 43, 56, 45, 66, 57, 17, 44, 74, 47, 67, 18, 69, 46, 49, 68, 19, 70,
        48, 51, 50, 71,
    ),
)


def _steps():
    qs, ns, two = range(6), range(2), range(2)
    steps = [("ws", q) for q in qs] + [("ts", a) for a in two]
    steps += [("wo", n, q) for n in ns for q in qs]
    steps += [("tn", n, cc, a) for n in ns for cc in two for a in two]
    steps += [("wn", n, q, way) for n in ns for q in qs for way in two]
    steps += [("tx", n, cc, a) for n in ns for cc in two for a in two]
    steps += [("wl", n, q) for n in ns for q in qs] + [("tw", n, cc) for n in ns for cc in two]
    return steps


STEPS = _steps()


def mod(a, n):
    return lax.rem(a + 2 * n, n)


def coords():
    dp = lax.axis_index("dp")
    t = lax.axis_index("tensor")
    z_hi, y = dp // 4, lax.rem(dp, 4)
    z_lo, x, c = t // 8, lax.rem(t // 2, 4), lax.rem(t, 2)
    return x, y, 2 * z_hi + z_lo, c


def device(x, y, z, c):
    if isinstance(z, int):
        return ((z // 2) * 4 + y, (z % 2) * 8 + x * 2 + c)
    return ((z // 2) * 4 + y, lax.rem(z, 2) * 8 + x * 2 + c)


def carried(z, c):
    z_hi, z_lo = z // 2, z % 2
    s = (c + z_hi) % 2
    zs = ((z_hi + s) % 4, (z_hi + s + 2) % 4)
    return zs[::-1] if s and z_lo == 0 else zs


def gather_kernel(
    li, og, wg, wu, wd, po, pin, gain, lens,
    out,
    tok, bwg, bwu, bwd, bpo, acc_g, acc_u, acc_b, acc_l, acc_o, src_n, src_g, sq_mine, sq_all,
    r_tok, r_w, r_po, r_sq, s_all, s_po, s_sq,
):
    x, y, z, c = coords()
    z_hi, z_lo = z // 2, lax.rem(z, 2)
    xp, xm, yp, ym = mod(x + 1, 4), mod(x - 1, 4), mod(y + 1, 4), mod(y - 1, 4)
    other = (x, y, z, 1 - c)
    z1 = mod(z + 1 - 2 * z_lo, 8)
    ka, kc = lax.rem(z_hi, 2), z_hi // 2

    barrier = pltpu.get_barrier_semaphore()
    peers = [(x, yp, z, c), (x, ym, z, c), other]
    for dz in range(1, 8):
        for cc in (0, 1):
            peers.append((x, y, mod(z + dz, 8), cc))
    for dx in range(1, 4):
        for zz in (z, z1):
            for cc in (0, 1):
                peers.append((mod(x + dx, 4), y, zz, cc))
    for p in peers:
        pl.semaphore_signal(barrier, inc=1, device_id=device(*p), device_id_type=MESH)
    pl.semaphore_wait(barrier, len(peers))

    def remote(src, dst, ssem, rsem, to):
        return pltpu.make_async_remote_copy(
            src_ref=src, dst_ref=dst, send_sem=ssem, recv_sem=rsem,
            device_id=device(*to), device_id_type=MESH,
        )

    def arrived(ref, sem):
        pltpu.make_async_copy(ref, ref, sem).wait()

    chunks = [(0, 0), (1, 0), (2, 0), (0, 1), (1, 1), (2, 1)]

    def wslot(j, q):
        m, h = chunks[q]
        n = KB // 2 if m < 2 else HID // 2
        return (bwg, bwu, bwd)[m].at[j, pl.ds(h * n, n)]

    def wsrc(q):
        m, h = chunks[q]
        n = KB // 2 if m < 2 else HID // 2
        return (wg, wu, wd)[m].at[pl.ds(h * n, n)]

    def walk(z, c, numbers, first, drain):
        z_hi, z_lo = z // 2, z % 2
        ka, z1 = z_hi % 2, z ^ 1
        zs = carried(z, c)
        kt = z_lo + 2 * c
        rel, f = (z_hi - kt) % 4, z_hi % 2
        entry = 1 if rel == 1 else 0 if rel == 3 else 1 - z_lo
        far = z1 if rel == 0 else 2 * kt + entry
        b, i = z_hi % 2, z_hi // 2
        hop = 2 if z_lo == b else 1
        r0 = (z - 2 * z_lo - 4 * c) % 8
        u0 = 1 - ((r0 + 7) % 8) // 4
        us = (u0, 1 - u0)
        count = [first]

        def send(src, dst, rsem, to):
            d = remote(src, dst, s_all.at[count[0]], rsem, to)
            count[0] += 1
            d.wait_send() if drain else d.start()

        def await_(ref, sem):
            if not drain:
                arrived(ref, sem)

        for number in numbers:
            kind, *arg = STEPS[number]
            if kind == "ws":
                j, q = z_hi * 4 + y, arg[0]
                if rel == 0 and f != c:
                    send(wsrc(q), wslot(j, q), r_w.at[j, q], (x, y, z, 1 - c))
                if rel == 0 and f == c and not drain:
                    pltpu.make_async_copy(wsrc(q), wslot(j, q), r_w.at[j, q]).start()
                send(wsrc(q), wslot(j, q), r_w.at[j, q], (x, y, far, f))
            elif kind == "ts":
                a = arg[0]
                j = z_lo * 8 + x * 2 + c
                src, dst, sem = (src_n, src_g)[a], tok.at[a, j], r_tok.at[a, j]
                if hop == 2 and i != c:
                    send(src, dst, sem, (x, y, z, i))
                if hop == 2 and i == c and not drain:
                    pltpu.make_async_copy(src, dst, sem).start()
                send(src, dst, sem, (x, y, (z + hop) % 8, i))
                send(src, dst, sem, (x, y, (z - hop) % 8, i))
            elif kind == "wo":
                n, q = arg
                j, r = zs[n] * 4 + y, (zs[n] - z_hi) % 4
                ent = 1 if r == 1 else 0 if r == 3 else 1 - ka
                blk, sem = wslot(j, q), r_w.at[j, q]
                await_(blk, sem)
                if r != 0 and z_lo == ent:
                    send(blk, blk, sem, (x, y, z1, c))
                send(blk, blk, sem, (x, yp, z, c))
                send(blk, blk, sem, (x, ym, z, c))
                send(blk, blk, sem, (x, y, z, 1 - c))
            elif kind == "wn":
                n, q, way = arg
                j = zs[n] * 4 + (ym, yp)[way]
                blk, sem = wslot(j, q), r_w.at[j, q]
                await_(blk, sem)
                if q // 3 == way:
                    send(blk, blk, sem, (x, (yp, ym)[way], z, c))
                send(blk, blk, sem, (x, y, z, 1 - c))
            elif kind == "wl":
                n, q = arg
                j = zs[n] * 4 + mod(y + 2, 4)
                blk, sem = wslot(j, q), r_w.at[j, q]
                await_(blk, sem)
                send(blk, blk, sem, (x, y, z, 1 - c))
            elif kind == "tn":
                n, cc, a = arg
                u = us[n]
                r = (r0 - u) % 8
                j = u * 8 + x * 2 + cc
                blk, sem = tok.at[a, j], r_tok.at[a, j]
                await_(blk, sem)
                if r in ((1, 2), (1,))[a]:
                    send(blk, blk, sem, (x, y, (z + 2) % 8, c))
                if r in ((7,), (6, 7))[a]:
                    send(blk, blk, sem, (x, y, (z - 2) % 8, c))
                send(blk, blk, sem, (xp, y, z, c))
                send(blk, blk, sem, (xm, y, z, c))
            elif kind == "tx":
                n, cc, a = arg
                j = us[n] * 8 + (xm, xp)[a] * 2 + cc
                blk, sem = tok.at[a, j], r_tok.at[a, j]
                await_(blk, sem)
                send(blk, blk, sem, ((xp, xm)[a], y, z, c))
            elif kind == "tw":
                n, cc = arg
                for a in (0, 1):
                    for xx in ((xp, xm)[a], mod(x + 2, 4)):
                        j = us[n] * 8 + xx * 2 + cc
                        await_(tok.at[a, j], r_tok.at[a, j])
        return count[0]

    sent = {}

    def everyone(part, drain=False):
        for zz in range(8):
            for cc in range(2):
                order = ORDERS[zz * 2 + cc]
                cut = min(order.index(n) for n, s in enumerate(STEPS) if s[0] == "ts")
                numbers = (order[:cut], order[cut:])[part]
                first = sent[zz, cc] if part else 0

                def go(zz=zz, cc=cc, numbers=numbers, first=first):
                    sent[zz, cc] = walk(zz, cc, numbers, first, drain)

                pl.when((z == zz) & (c == cc))(go)

    v = li[...].astype(F32)
    ones = jnp.ones((8, KB), F32)
    row = lax.dot_general(
        ones, v * v, (((1,), (1,)), ((), ())), precision=lax.Precision.HIGHEST, preferred_element_type=F32
    )
    sq_mine[...] = row[0:1, :]
    t_me = z_lo * 8 + x * 2 + c
    sq_sends = []
    for d in range(1, 16):
        to = (mod(x + (d // 2) % 4, 4), y, (z, z1)[d // 8], lax.rem(c + d % 2, 2))
        sq_sends.append(remote(sq_mine, sq_all.at[t_me], s_sq.at[d], r_sq.at[t_me], to))
        sq_sends[-1].start()
    everyone(0)

    has_po = (z_lo == ka) & (c == kc)
    po_sends = [
        remote(po, bpo, s_po.at[0], r_po, other),
        remote(po, bpo, s_po.at[1], r_po, (x, y, z1, 0)),
        remote(po, bpo, s_po.at[2], r_po, (x, y, z1, 1)),
    ]

    def start_po():
        for d in po_sends:
            d.start()
        pltpu.make_async_copy(po, bpo, r_po).start()

    pl.when(has_po)(start_po)

    at = lax.broadcasted_iota(jnp.int32, (TOK, KB), 0)
    count = jnp.where(at < TOK // 2, lens[0, 0], lens[0, 1])
    valid = (at % (TOK // 2)) < count
    src_g[...] = jnp.where(valid, og[...].astype(F32), 0.0).astype(BF16)
    total = row[0:1, :]
    for d in range(1, 16):
        t = lax.rem(z_lo + d // 8, 2) * 8 + mod(x + (d // 2) % 4, 4) * 2 + lax.rem(c + d % 2, 2)
        arrived(sq_all.at[t], r_sq.at[t])
        total = total + sq_all[t]
    factor = lax.rsqrt(total * (1.0 / 4096.0) + 1e-05)
    factor = jnp.transpose(jnp.broadcast_to(factor, (8, TOK)), (1, 0))[:, 0:1]
    src_n[...] = (v * factor * gain[t_me]).astype(BF16)

    everyone(1)
    arrived(bpo, r_po)

    for ref in (acc_g, acc_u, acc_b, acc_l, acc_o):
        ref[...] = jnp.zeros_like(ref)
    carry = lax.rem(c + z_hi, 2)

    @pl.loop(0, NB)
    def _(s):
        rest = s // 8
        zz = mod(z_hi + carry + rest + 2 * (lax.rem(s, 8) // 4), 4)
        j = zz * 4 + mod(y + lax.rem(s, 4), 4)

        def wait_rest():
            for q in range(6):
                arrived(wslot(j, q), r_w.at[j, q])

        pl.when(rest == 1)(wait_rest)
        n = tok[0, j]
        acc_g[...] += jnp.dot(n, bwg[j], preferred_element_type=F32)
        acc_u[...] += jnp.dot(n, bwu[j], preferred_element_type=F32)
        acc_l[...] += jnp.dot(n, pin[j], preferred_element_type=F32)
        acc_b[...] += lax.dot_general(
            tok[1, j], bwd[j], (((1,), (1,)), ((), ())), preferred_element_type=F32
        )

    @pl.loop(0, TOK // 128)
    def _(t):
        rows = pl.ds(pl.multiple_of(t * 128, 128), 128)
        gate = acc_g[rows, :]
        sig = 1.0 / (1.0 + jnp.exp(-gate))
        dgate = (acc_b[rows, :] * acc_u[rows, :] * sig * (1.0 + gate * (1.0 - sig))).astype(BF16)
        right = lax.dot_general(
            dgate, bpo[...], (((1,), (1,)), ((), ())), preferred_element_type=F32
        )
        acc_o[...] += lax.dot_general(
            acc_l[rows, :], right, (((0,), (0,)), ((), ())),
            precision=lax.Precision.HIGHEST, preferred_element_type=F32,
        )

    for j in range(NB):
        out[j] = acc_o[4 * j:4 * j + 4, :]

    everyone(0, drain=True)
    everyone(1, drain=True)
    for d in sq_sends:
        d.wait_send()

    def wait_po():
        for d in po_sends:
            d.wait_send()

    pl.when(has_po)(wait_po)


def finish_kernel(part, q, grad, score, got1, mine, got2, got3, got4, rows, r1, r2, r3, r4, s1, s2, s3, s4):
    x, y, z, c = coords()
    z_hi, z_lo = z // 2, lax.rem(z, 2)
    ph = z_lo + 2 * c
    piece = z_hi * 4 + x

    def dev2(zh, yy, zl, xx, cc):
        return (zh * 4 + yy, zl * 8 + xx * 2 + cc)

    team = [(mod(z_hi + d // 4, 4), mod(x + d % 4, 4)) for d in range(1, 16)]
    same_t = [(mod(z_hi + d // 4, 4), mod(y + d % 4, 4)) for d in range(1, 16)]
    every_t = [(lax.rem(z_lo + d // 8, 2), mod(x + (d // 2) % 4, 4), lax.rem(c + d % 2, 2)) for d in range(16)]
    barrier = pltpu.get_barrier_semaphore()

    def tell(to):
        pl.semaphore_signal(barrier, inc=1, device_id=to, device_id_type=MESH)

    for zh, xx in team:
        tell(dev2(zh, y, z_lo, xx, c))
    for zh, yy in same_t:
        tell(dev2(zh, yy, z_lo, x, c))
    for d in range(16):
        tell(dev2(d // 4, y, lax.rem(z_hi, 2), d % 4, z_hi // 2))
        tell(dev2(z_hi, d // 4, d % 2, y, (d // 2) % 2))
    pl.semaphore_wait(barrier, 62)
    waits = []

    def send(src, dst, ssem, rsem, to, self_=None):
        d = pltpu.make_async_remote_copy(
            src_ref=src, dst_ref=dst, send_sem=ssem, recv_sem=rsem, device_id=to, device_id_type=MESH,
        )
        if self_ is None:
            d.start()
            waits.append(d.wait_send)
        else:
            def stay():
                pltpu.make_async_copy(src, dst, rsem).start()

            pl.when(jnp.logical_not(self_))(lambda: d.start())
            pl.when(self_)(stay)
            waits.append(lambda: pl.when(jnp.logical_not(self_))(lambda: d.wait_send()))

    def arrived(ref, sem):
        pltpu.make_async_copy(ref, ref, sem).wait()

    for n, (zh, xx) in enumerate(team):
        send(part.at[zh * 4 + xx], got1.at[piece], s1.at[n], r1.at[piece], dev2(zh, y, z_lo, xx, c))
    total = part[piece]
    for zh, xx in team:
        m = zh * 4 + xx
        arrived(got1.at[m], r1.at[m])
        total = total + got1[m]
    mine[...] = total
    pair = ph * 4 + y
    for n, (zl, xx, cc) in enumerate(every_t):
        send(mine, got3.at[pair], s3.at[n], r3.at[pair], dev2(z_hi, x, zl, xx, cc), (x == y) if n == 0 else None)
    for n, (zl, xx, cc) in enumerate(every_t):
        send(mine, got2.at[piece], s2.at[n], r2.at[piece], dev2(ph, y, zl, xx, cc), (ph == z_hi) if n == 0 else None)
    for p in range(16):
        arrived(got3.at[p], r3.at[p])
    s = jnp.zeros((16, KB), F32)
    for r in range(4):
        f = got3[:, r, :].astype(BF16)
        s = s + lax.dot_general(
            f, q[:, r * RANK:(r + 1) * RANK], (((1,), (1,)), ((), ())), preferred_element_type=F32
        )
    for p in range(16):
        rows[p] = s[p:p + 1, :]
    me = z_hi * 4 + y
    for n, (zh, yy) in enumerate(same_t):
        send(rows.at[zh * 4 + yy], got4.at[me], s4.at[n], r4.at[me], dev2(zh, yy, z_lo, x, c))
    for p in range(16):
        arrived(got2.at[p], r2.at[p])
        grad[p] = got2[p]
    total = rows[me]
    for zh, yy in same_t:
        m = zh * 4 + yy
        arrived(got4.at[m], r4.at[m])
        total = total + got4[m]
    score[...] = total
    for w in waits:
        w()


def finish(part, queries):
    vmem = pl.BlockSpec(memory_space=pltpu.VMEM)
    dma = pltpu.SemaphoreType.DMA
    piece = pltpu.VMEM((NB, 4, RANK), F32)
    row = pltpu.VMEM((16, 1, KB), F32)
    return pl.pallas_call(
        finish_kernel,
        out_shape=(
            jax.ShapeDtypeStruct((NB, 4, RANK), F32),
            jax.ShapeDtypeStruct((1, KB), F32),
        ),
        in_specs=[vmem] * 2,
        out_specs=(vmem, vmem),
        scratch_shapes=[piece, pltpu.VMEM((4, RANK), F32), piece, piece, row, row]
        + [dma((16,))] * 8,
        compiler_params=pltpu.CompilerParams(collective_id=1, has_side_effects=True),
    )(part, queries)


def gathered(li, og, wg, wu, wd, po, pin, gain, lens):
    any_ = pl.BlockSpec(memory_space=pl.ANY)
    vmem = pl.BlockSpec(memory_space=pltpu.VMEM)
    smem = pl.BlockSpec(memory_space=pltpu.SMEM)
    dma = pltpu.SemaphoreType.DMA
    return pl.pallas_call(
        gather_kernel,
        out_shape=jax.ShapeDtypeStruct((NB, 4, RANK), F32),
        in_specs=[vmem] * 2 + [any_] * 4 + [vmem] * 2 + [smem],
        out_specs=vmem,
        scratch_shapes=[
            pltpu.VMEM((2, NB, TOK, KB), BF16),
            pltpu.VMEM((NB, KB, HID), BF16),
            pltpu.VMEM((NB, KB, HID), BF16),
            pltpu.VMEM((NB, HID, KB), BF16),
            pltpu.VMEM((RANK, HID), BF16),
            pltpu.VMEM((TOK, HID), F32),
            pltpu.VMEM((TOK, HID), F32),
            pltpu.VMEM((TOK, HID), F32),
            pltpu.VMEM((TOK, RANK), F32),
            pltpu.VMEM((RANK, RANK), F32),
            pltpu.VMEM((TOK, KB), BF16),
            pltpu.VMEM((TOK, KB), BF16),
            pltpu.VMEM((1, TOK), F32),
            pltpu.VMEM((16, 1, TOK), F32),
            dma((2, NB)),
            dma((NB, 6)),
            dma,
            dma((16,)),
            dma((NSEND,)),
            dma((3,)),
            dma((16,)),
        ],
        compiler_params=pltpu.CompilerParams(
            collective_id=0, has_side_effects=True, vmem_limit_bytes=60 << 20
        ),
    )(li, og, wg, wu, wd, po, pin, gain, lens)


def on_device(
    layer_input,
    out_grad,
    norm_gain,
    gate_weight,
    up_weight,
    down_weight,
    lengths,
    proj_in,
    proj_out,
    queries,
):
    part = gathered(
        layer_input.reshape(TOK, KB),
        out_grad.reshape(TOK, KB),
        gate_weight,
        up_weight,
        down_weight,
        proj_out.T,
        proj_in.reshape(NB, KB, RANK),
        norm_gain.reshape(NB, 1, KB),
        lengths,
    )
    grad, scores = finish(part, queries)
    return (grad.reshape(1, RANK, RANK), scores)


def solution(mesh):
    in_specs = (
        P("dp", None, None, "tensor"),
        P("dp", None, None, "tensor"),
        P(),
        P("dp", "tensor"),
        P("dp", "tensor"),
        P("tensor", "dp"),
        P("dp", None),
        P(),
        P("tensor", None),
        P("tensor", "dp"),
    )
    out_specs = (P("dp", None, None), P("dp", "tensor"))
    return jax.shard_map(
        on_device, mesh=mesh, in_specs=in_specs, out_specs=out_specs, check_vma=False
    )
```

time: 221 us -> 178 us (0.81)
  Pallas kernels: 210 us -> 172 us
  other arithmetic: 2.58 us -> 0 us
    pallas_call x1, Pallas kernels: 169 us -> 126 us  [gathered(): pl.pallas_call(gather_kernel, out_shape=jax.ShapeDtypeStruct((NB, 4, RANK...]
    pallas_call x1, Pallas kernels: 41.2 us -> 46.2 us  [finish(): pl.pallas_call(finish_kernel, out_shape=(jax.ShapeDtypeStruct((NB, 4, RAN...]
    unnamed x8 -> x5, local copies, waits for them, and re-layouts: 5.01 us -> 4.31 us
where the time goes in v3:
time: 178 us; the launch traced here: 177 us
  Pallas kernels  172 us (97%)
  local copies, waits for them, and re-layouts  4.31 us (2%)
    pallas_call x1, Pallas kernels, gathered(): pl.pallas_call(gather_kernel, out_shape=jax.ShapeDtypeStruct((NB, 4, RANK...  126 us
    pallas_call x1, Pallas kernels, finish(): pl.pallas_call(finish_kernel, out_shape=(jax.ShapeDtypeStruct((NB, 4, RAN...  46.2 us
    unnamed x5, local copies, waits for them, and re-layouts  4.31 us

profile of v3, /device:TPU:32, one launch (start us, length us, event | category | flops | bytes accessed | tf_op | source)
XLA Modules:
  0.0 176.8 jit_solution(7447843573849488022)
XLA Ops:
  0.6 2.4 %copy.12 = bf16[4096,64]{1,0:T(8,128)(2,1)} copy(bf16[4096,64]{0,1:T(8,128)(2,1)} %param.17) | data formatting | bytes 1048576 | tf_op args[7]
  3.0 125.7 %shard_map.113.part = f32[16,4,64]{2,1,0:T(4,128)} custom-call(bf16[512,256]{1,0:T(8,128)(2,1)} %bitcast.7, bf16[512,256]{1,0:T(8,128)(2,1)} %bitcast.8, bf16[256,896]{1,0:T(8,128)(2,1)} %wg.1, bf16[256,896]{1,0:T(8,128)(2,1)} %wu.1, bf16[896,256]{1,0:T(8,128)(2,1)} %wd.1, bf16[64,896]{1,0:T(8,128)(2,1)} %bitcast.9, bf16[16,256,64]{2,1,0:T(8,128)(2,1)} %bitcast.6, ...), custom_call_target="tpu_custom_call" | custom-call | tf_op jit(solution)/shard_map/pallas_call | solution.py:518
  128.7 46.2 %shard_map.114 = (f32[16,4,64]{2,1,0:T(4,128)}, f32[1,256]{1,0:T(1,128)}) custom-call(f32[16,4,64]{2,1,0:T(4,128)} %shard_map.113.part, bf16[256,256]{1,0:T(8,128)(2,1)} %q.1), custom_call_target="tpu_custom_call" | custom-call | tf_op jit(solution)/shard_map/pallas_call | solution.py:499
  174.8 0.0 copy-start
  174.8 1.4 copy.15
  176.2 0.0 copy-done
  176.2 0.6 copy.16
Async XLA Ops:
  174.8 1.4 copy-start

commit v4 on v3

--- a/solution.py
+++ b/solution.py
@@ -147,6 +147,10 @@
     return ((z // 2) * 4 + y, lax.rem(z, 2) * 8 + x * 2 + c)
 
 
+def at5(zh, yy, zl, xx, cc):
+    return (zh * 4 + yy, zl * 8 + xx * 2 + cc)
+
+
 def carried(z, c):
     z_hi, z_lo = z // 2, z % 2
     s = (c + z_hi) % 2
@@ -155,10 +159,11 @@
 
 
 def gather_kernel(
-    li, og, wg, wu, wd, po, pin, gain, lens,
-    out,
+    li, og, wg, wu, wd, po, pin, gain, lens, q,
+    grad, score,
     tok, bwg, bwu, bwd, bpo, acc_g, acc_u, acc_b, acc_l, acc_o, src_n, src_g, sq_mine, sq_all,
-    r_tok, r_w, r_po, r_sq, s_all, s_po, s_sq,
+    part, got1, mine, got2, got3, got4, rows4,
+    r_tok, r_w, r_po, r_sq, s_all, s_po, s_sq, r1, r2, r3, r4, s1, s2, s3, s4,
 ):
     x, y, z, c = coords()
     z_hi, z_lo = z // 2, lax.rem(z, 2)
@@ -176,9 +181,16 @@
         for zz in (z, z1):
             for cc in (0, 1):
                 peers.append((mod(x + dx, 4), y, zz, cc))
-    for p in peers:
-        pl.semaphore_signal(barrier, inc=1, device_id=device(*p), device_id_type=MESH)
-    pl.semaphore_wait(barrier, len(peers))
+    team = [(mod(z_hi + d // 4, 4), mod(x + d % 4, 4)) for d in range(1, 16)]
+    same_t = [(mod(z_hi + d // 4, 4), mod(y + d % 4, 4)) for d in range(1, 16)]
+    ends = [(zh, y, z_lo, xx, c) for zh, xx in team] + [(zh, yy, z_lo, x, c) for zh, yy in same_t]
+    for d in range(16):
+        ends.append((d // 4, y, lax.rem(z_hi, 2), d % 4, z_hi // 2))
+        ends.append((z_hi, d // 4, d % 2, y, (d // 2) % 2))
+    signals = [device(*p) for p in peers] + [at5(*p) for p in ends]
+    for p in signals:
+        pl.semaphore_signal(barrier, inc=1, device_id=p, device_id_type=MESH)
+    pl.semaphore_wait(barrier, len(signals))
 
     def remote(src, dst, ssem, rsem, to):
         return pltpu.make_async_remote_copy(
@@ -355,28 +367,40 @@
     everyone(1)
     arrived(bpo, r_po)
 
-    for ref in (acc_g, acc_u, acc_b, acc_l, acc_o):
-        ref[...] = jnp.zeros_like(ref)
     carry = lax.rem(c + z_hi, 2)
 
-    @pl.loop(0, NB)
+    def product(s, first):
+        rest = s // 2
+        zz = mod(z_hi + carry + rest + 2 * lax.rem(s, 2), 4)
+
+        def wait_rest():
+            for dy in range(4):
+                j = zz * 4 + dy
+                for q in range(6):
+                    arrived(wslot(j, q), r_w.at[j, q])
+
+        pl.when(rest == 1)(wait_rest)
+        js = pl.ds(zz * 4, 4)
+        n = jnp.concatenate([tok[0, zz * 4 + k] for k in range(4)], axis=1)
+        g = jnp.concatenate([tok[1, zz * 4 + k] for k in range(4)], axis=1)
+        down = jnp.concatenate([bwd[zz * 4 + k] for k in range(4)], axis=1)
+
+        def add(acc, value):
+            acc[...] = value if first else acc[...] + value
+
+        add(acc_g, jnp.dot(n, bwg[js].reshape(4 * KB, HID), preferred_element_type=F32))
+        add(acc_u, jnp.dot(n, bwu[js].reshape(4 * KB, HID), preferred_element_type=F32))
+        cols = pl.ds(pl.multiple_of(zz * (4 * KB), 4 * KB), 4 * KB)
+        add(acc_l, lax.dot_general(n, pin[:, cols], (((1,), (1,)), ((), ())), preferred_element_type=F32))
+        add(acc_b, lax.dot_general(g, down, (((1,), (1,)), ((), ())), preferred_element_type=F32))
+
+    product(0, True)
+
+    @pl.loop(1, 4)
     def _(s):
-        rest = s // 8
-        zz = mod(z_hi + carry + rest + 2 * (lax.rem(s, 8) // 4), 4)
-        j = zz * 4 + mod(y + lax.rem(s, 4), 4)
-
-        def wait_rest():
-            for q in range(6):
-                arrived(wslot(j, q), r_w.at[j, q])
-
-        pl.when(rest == 1)(wait_rest)
-        n = tok[0, j]
-        acc_g[...] += jnp.dot(n, bwg[j], preferred_element_type=F32)
-        acc_u[...] += jnp.dot(n, bwu[j], preferred_element_type=F32)
-        acc_l[...] += jnp.dot(n, pin[j], preferred_element_type=F32)
-        acc_b[...] += lax.dot_general(
-            tok[1, j], bwd[j], (((1,), (1,)), ((), ())), preferred_element_type=F32
-        )
+        product(s, False)
+
+    acc_o[...] = jnp.zeros_like(acc_o)
 
     @pl.loop(0, TOK // 128)
     def _(t):
@@ -393,8 +417,32 @@
         )
 
     for j in range(NB):
-        out[j] = acc_o[4 * j:4 * j + 4, :]
-
+        part[j] = acc_o[4 * j:4 * j + 4, :]
+
+    ph = z_lo + 2 * c
+    piece = z_hi * 4 + x
+    pair = ph * 4 + y
+    me = z_hi * 4 + y
+    every_t = [(lax.rem(z_lo + d // 8, 2), mod(x + (d // 2) % 4, 4), lax.rem(c + d % 2, 2)) for d in range(16)]
+    last = []
+
+    def send5(src, dst, ssem, rsem, to, stays=None):
+        d = pltpu.make_async_remote_copy(
+            src_ref=src, dst_ref=dst, send_sem=ssem, recv_sem=rsem, device_id=at5(*to), device_id_type=MESH,
+        )
+        if stays is None:
+            d.start()
+            last.append(d.wait_send)
+        else:
+            def stay():
+                pltpu.make_async_copy(src, dst, rsem).start()
+
+            pl.when(jnp.logical_not(stays))(lambda: d.start())
+            pl.when(stays)(stay)
+            last.append(lambda: pl.when(jnp.logical_not(stays))(lambda: d.wait_send()))
+
+    for n, (zh, xx) in enumerate(team):
+        send5(part.at[zh * 4 + xx], got1.at[piece], s1.at[n], r1.at[piece], (zh, y, z_lo, xx, c))
     everyone(0, drain=True)
     everyone(1, drain=True)
     for d in sq_sends:
@@ -405,66 +453,16 @@
             d.wait_send()
 
     pl.when(has_po)(wait_po)
-
-
-def finish_kernel(part, q, grad, score, got1, mine, got2, got3, got4, rows, r1, r2, r3, r4, s1, s2, s3, s4):
-    x, y, z, c = coords()
-    z_hi, z_lo = z // 2, lax.rem(z, 2)
-    ph = z_lo + 2 * c
-    piece = z_hi * 4 + x
-
-    def dev2(zh, yy, zl, xx, cc):
-        return (zh * 4 + yy, zl * 8 + xx * 2 + cc)
-
-    team = [(mod(z_hi + d // 4, 4), mod(x + d % 4, 4)) for d in range(1, 16)]
-    same_t = [(mod(z_hi + d // 4, 4), mod(y + d % 4, 4)) for d in range(1, 16)]
-    every_t = [(lax.rem(z_lo + d // 8, 2), mod(x + (d // 2) % 4, 4), lax.rem(c + d % 2, 2)) for d in range(16)]
-    barrier = pltpu.get_barrier_semaphore()
-
-    def tell(to):
-        pl.semaphore_signal(barrier, inc=1, device_id=to, device_id_type=MESH)
-
-    for zh, xx in team:
-        tell(dev2(zh, y, z_lo, xx, c))
-    for zh, yy in same_t:
-        tell(dev2(zh, yy, z_lo, x, c))
-    for d in range(16):
-        tell(dev2(d // 4, y, lax.rem(z_hi, 2), d % 4, z_hi // 2))
-        tell(dev2(z_hi, d // 4, d % 2, y, (d // 2) % 2))
-    pl.semaphore_wait(barrier, 62)
-    waits = []
-
-    def send(src, dst, ssem, rsem, to, self_=None):
-        d = pltpu.make_async_remote_copy(
-            src_ref=src, dst_ref=dst, send_sem=ssem, recv_sem=rsem, device_id=to, device_id_type=MESH,
-        )
-        if self_ is None:
-            d.start()
-            waits.append(d.wait_send)
-        else:
-            def stay():
-                pltpu.make_async_copy(src, dst, rsem).start()
-
-            pl.when(jnp.logical_not(self_))(lambda: d.start())
-            pl.when(self_)(stay)
-            waits.append(lambda: pl.when(jnp.logical_not(self_))(lambda: d.wait_send()))
-
-    def arrived(ref, sem):
-        pltpu.make_async_copy(ref, ref, sem).wait()
-
-    for n, (zh, xx) in enumerate(team):
-        send(part.at[zh * 4 + xx], got1.at[piece], s1.at[n], r1.at[piece], dev2(zh, y, z_lo, xx, c))
     total = part[piece]
     for zh, xx in team:
         m = zh * 4 + xx
         arrived(got1.at[m], r1.at[m])
         total = total + got1[m]
     mine[...] = total
-    pair = ph * 4 + y
     for n, (zl, xx, cc) in enumerate(every_t):
-        send(mine, got3.at[pair], s3.at[n], r3.at[pair], dev2(z_hi, x, zl, xx, cc), (x == y) if n == 0 else None)
+        send5(mine, got3.at[pair], s3.at[n], r3.at[pair], (z_hi, x, zl, xx, cc), (x == y) if n == 0 else None)
     for n, (zl, xx, cc) in enumerate(every_t):
-        send(mine, got2.at[piece], s2.at[n], r2.at[piece], dev2(ph, y, zl, xx, cc), (ph == z_hi) if n == 0 else None)
+        send5(mine, got2.at[piece], s2.at[n], r2.at[piece], (ph, y, zl, xx, cc), (ph == z_hi) if n == 0 else None)
     for p in range(16):
         arrived(got3.at[p], r3.at[p])
     s = jnp.zeros((16, KB), F32)
@@ -474,52 +472,37 @@
             f, q[:, r * RANK:(r + 1) * RANK], (((1,), (1,)), ((), ())), preferred_element_type=F32
         )
     for p in range(16):
-        rows[p] = s[p:p + 1, :]
-    me = z_hi * 4 + y
+        rows4[p] = s[p:p + 1, :]
     for n, (zh, yy) in enumerate(same_t):
-        send(rows.at[zh * 4 + yy], got4.at[me], s4.at[n], r4.at[me], dev2(zh, yy, z_lo, x, c))
+        send5(rows4.at[zh * 4 + yy], got4.at[me], s4.at[n], r4.at[me], (zh, yy, z_lo, x, c))
     for p in range(16):
         arrived(got2.at[p], r2.at[p])
-        grad[p] = got2[p]
-    total = rows[me]
+        grad[4 * p:4 * p + 4, :] = got2[p]
+    total = rows4[me]
     for zh, yy in same_t:
         m = zh * 4 + yy
         arrived(got4.at[m], r4.at[m])
         total = total + got4[m]
     score[...] = total
-    for w in waits:
+    for w in last:
         w()
 
 
-def finish(part, queries):
+def gathered(li, og, wg, wu, wd, po, pin, gain, lens, q):
+    any_ = pl.BlockSpec(memory_space=pl.ANY)
     vmem = pl.BlockSpec(memory_space=pltpu.VMEM)
+    smem = pl.BlockSpec(memory_space=pltpu.SMEM)
     dma = pltpu.SemaphoreType.DMA
     piece = pltpu.VMEM((NB, 4, RANK), F32)
     row = pltpu.VMEM((16, 1, KB), F32)
     return pl.pallas_call(
-        finish_kernel,
+        gather_kernel,
         out_shape=(
-            jax.ShapeDtypeStruct((NB, 4, RANK), F32),
+            jax.ShapeDtypeStruct((RANK, RANK), F32),
             jax.ShapeDtypeStruct((1, KB), F32),
         ),
-        in_specs=[vmem] * 2,
+        in_specs=[vmem] * 2 + [any_] * 4 + [vmem] * 2 + [smem, vmem],
         out_specs=(vmem, vmem),
-        scratch_shapes=[piece, pltpu.VMEM((4, RANK), F32), piece, piece, row, row]
-        + [dma((16,))] * 8,
-        compiler_params=pltpu.CompilerParams(collective_id=1, has_side_effects=True),
-    )(part, queries)
-
-
-def gathered(li, og, wg, wu, wd, po, pin, gain, lens):
-    any_ = pl.BlockSpec(memory_space=pl.ANY)
-    vmem = pl.BlockSpec(memory_space=pltpu.VMEM)
-    smem = pl.BlockSpec(memory_space=pltpu.SMEM)
-    dma = pltpu.SemaphoreType.DMA
-    return pl.pallas_call(
-        gather_kernel,
-        out_shape=jax.ShapeDtypeStruct((NB, 4, RANK), F32),
-        in_specs=[vmem] * 2 + [any_] * 4 + [vmem] * 2 + [smem],
-        out_specs=vmem,
         scratch_shapes=[
             pltpu.VMEM((2, NB, TOK, KB), BF16),
             pltpu.VMEM((NB, KB, HID), BF16),
@@ -535,6 +518,7 @@
             pltpu.VMEM((TOK, KB), BF16),
             pltpu.VMEM((1, TOK), F32),
             pltpu.VMEM((16, 1, TOK), F32),
+            piece, piece, pltpu.VMEM((4, RANK), F32), piece, piece, row, row,
             dma((2, NB)),
             dma((NB, 6)),
             dma,
@@ -542,11 +526,12 @@
             dma((NSEND,)),
             dma((3,)),
             dma((16,)),
+            *([dma((16,))] * 8),
         ],
         compiler_params=pltpu.CompilerParams(
             collective_id=0, has_side_effects=True, vmem_limit_bytes=60 << 20
         ),
-    )(li, og, wg, wu, wd, po, pin, gain, lens)
+    )(li, og, wg, wu, wd, po, pin, gain, lens, q)
 
 
 def on_device(
@@ -561,18 +546,18 @@
     proj_out,
     queries,
 ):
-    part = gathered(
+    grad, scores = gathered(
         layer_input.reshape(TOK, KB),
         out_grad.reshape(TOK, KB),
         gate_weight,
         up_weight,
         down_weight,
         proj_out.T,
-        proj_in.reshape(NB, KB, RANK),
+        proj_in.T,
         norm_gain.reshape(NB, 1, KB),
         lengths,
+        queries,
     )
-    grad, scores = finish(part, queries)
     return (grad.reshape(1, RANK, RANK), scores)
 
 

time: 178 us -> 161 us (0.904)
  Pallas kernels: 172 us -> 158 us
  local copies, waits for them, and re-layouts: 4.31 us -> 1.94 us
    pallas_call x2 -> x1, Pallas kernels: 172 us -> 158 us  [gathered(): pl.pallas_call(gather_kernel, out_shape=(jax.ShapeDtypeStruct((RANK, RANK...]
    unnamed x5 -> x4, local copies, waits for them, and re-layouts: 4.31 us -> 1.94 us
where the time goes in v4:
time: 161 us; the launch traced here: 160 us
  Pallas kernels  158 us (98%)
  local copies, waits for them, and re-layouts  1.94 us (1%)
    pallas_call x1, Pallas kernels, gathered(): pl.pallas_call(gather_kernel, out_shape=(jax.ShapeDtypeStruct((RANK, RANK...  158 us

profile of v4, /device:TPU:32, one launch (start us, length us, event | category | flops | bytes accessed | tf_op | source)
XLA Modules:
  0.0 160.1 jit_solution(16737035221247486450)
XLA Ops:
  0.6 157.5 %shard_map.113 = (f32[64,64]{1,0:T(8,128)}, f32[1,256]{1,0:T(1,128)}) custom-call(bf16[512,256]{1,0:T(8,128)(2,1)} %bitcast.7, bf16[512,256]{1,0:T(8,128)(2,1)} %bitcast.8, bf16[256,896]{1,0:T(8,128)(2,1)} %wg.1, bf16[256,896]{1,0:T(8,128)(2,1)} %wu.1, bf16[896,256]{1,0:T(8,128)(2,1)} %wd.1, bf16[64,896]{1,0:T(8,128)(2,1)} %bitcast.9, ...), custom_call_target="tpu_custom_call" | custom-call | tf_op jit(solution)/shard_map/pallas_call | solution.py:498
  158.2 0.0 copy-start
  158.2 1.4 copy.14
  159.6 0.0 copy-done
  159.6 0.6 copy.15
Async XLA Ops:
  158.2 1.4 copy-start

commit v5 on v4

--- a/solution.py
+++ b/solution.py
@@ -17,100 +17,100 @@
 
 ORDERS = (
     (
-        0, 1, 2, 3, 4, 5, 8, 9, 10, 11, 12, 13, 28, 29, 30, 31, 6, 7, 22, 20, 23, 21, 32, 33,
-        54, 24, 52, 34, 35, 55, 25, 53, 36, 37, 14, 38, 39, 56, 73, 57, 15, 60, 63, 72, 74, 61, 64, 41,
-        62, 16, 26, 40, 65, 42, 43, 27, 58, 44, 45, 59, 17, 66, 75, 18, 47, 67, 49, 68, 69, 46, 19, 70,
-        48, 51, 50, 71,
-    ),
-    (
-        0, 1, 2, 3, 4, 5, 8, 6, 7, 9, 28, 29, 10, 30, 31, 11, 33, 60, 12, 32, 35, 37, 61, 13,
-        34, 63, 14, 20, 27, 36, 64, 52, 24, 59, 39, 62, 38, 41, 21, 15, 65, 56, 40, 43, 16, 53, 42, 72,
-        17, 45, 66, 47, 44, 18, 22, 25, 67, 69, 54, 19, 57, 23, 46, 49, 74, 26, 68, 51, 55, 48, 58, 70,
-        50, 73, 75, 71,
-    ),
-    (
-        0, 1, 2, 3, 4, 5, 8, 6, 7, 14, 28, 29, 9, 41, 15, 40, 22, 31, 26, 60, 10, 43, 54, 16,
-        30, 33, 58, 23, 42, 27, 45, 11, 17, 66, 55, 35, 32, 59, 18, 12, 47, 44, 73, 20, 63, 19, 21, 61,
-        75, 52, 13, 49, 67, 37, 53, 34, 24, 69, 72, 46, 56, 25, 51, 62, 39, 48, 57, 70, 36, 74, 64, 68,
+        0, 1, 2, 3, 4, 5, 8, 9, 10, 11, 12, 13, 28, 6, 7, 30, 20, 22, 21, 23, 32, 29, 24, 31,
+        52, 35, 54, 33, 25, 53, 37, 34, 55, 14, 39, 36, 15, 56, 57, 72, 38, 60, 63, 73, 74, 61, 64, 16,
+        26, 40, 41, 62, 42, 27, 65, 44, 58, 43, 17, 59, 45, 47, 18, 66, 75, 67, 49, 69, 68, 19, 46, 51,
+        70, 48, 50, 71,
+    ),
+    (
+        0, 1, 2, 3, 4, 5, 8, 6, 7, 9, 28, 10, 30, 29, 11, 31, 12, 32, 35, 33, 60, 37, 13, 20,
+        61, 14, 27, 34, 63, 24, 52, 39, 59, 36, 64, 62, 21, 15, 40, 56, 38, 41, 16, 42, 65, 53, 17, 43,
+        44, 47, 72, 18, 22, 45, 66, 25, 19, 23, 54, 49, 57, 67, 69, 26, 51, 55, 46, 58, 74, 68, 48, 73,
+        70, 50, 75, 71,
+    ),
+    (
+        0, 1, 2, 3, 4, 5, 8, 6, 7, 14, 28, 9, 15, 40, 22, 29, 26, 41, 10, 16, 30, 31, 54, 60,
+        23, 42, 27, 43, 58, 11, 17, 33, 35, 55, 45, 32, 18, 66, 12, 47, 59, 44, 20, 19, 21, 73, 13, 49,
+        63, 52, 61, 75, 37, 53, 67, 24, 34, 25, 51, 56, 69, 72, 46, 39, 62, 57, 48, 70, 36, 74, 64, 68,
         71, 50, 65, 38,
     ),
     (
-        0, 1, 2, 3, 4, 5, 8, 6, 7, 28, 29, 9, 14, 60, 31, 22, 30, 10, 41, 54, 40, 33, 23, 11,
-        61, 35, 32, 55, 12, 63, 66, 26, 13, 73, 37, 34, 58, 15, 39, 62, 27, 64, 36, 16, 59, 43, 38, 24,
-        65, 20, 75, 42, 17, 45, 56, 44, 47, 25, 52, 67, 18, 21, 19, 69, 46, 57, 53, 49, 68, 74, 72, 51,
+        0, 1, 2, 3, 4, 5, 8, 6, 7, 28, 9, 14, 29, 22, 30, 10, 60, 40, 31, 54, 23, 11, 41, 35,
+        32, 33, 12, 61, 55, 26, 13, 37, 63, 66, 15, 39, 73, 58, 27, 34, 62, 16, 64, 59, 36, 24, 20, 42,
+        43, 38, 17, 44, 65, 75, 56, 47, 25, 18, 21, 45, 19, 52, 67, 57, 49, 53, 69, 46, 51, 68, 74, 72,
         48, 70, 50, 71,
     ),
     (
-        0, 1, 2, 3, 4, 5, 8, 6, 7, 9, 28, 29, 22, 30, 31, 10, 54, 60, 33, 23, 61, 11, 26, 55,
-        35, 32, 34, 63, 58, 12, 73, 27, 13, 62, 37, 20, 36, 59, 39, 21, 52, 38, 64, 14, 75, 65, 40, 53,
-        41, 66, 24, 72, 15, 16, 56, 17, 42, 43, 25, 18, 19, 44, 45, 57, 47, 46, 49, 67, 51, 74, 48, 69,
+        0, 1, 2, 3, 4, 5, 8, 6, 7, 28, 9, 22, 29, 10, 30, 54, 60, 31, 23, 32, 11, 26, 33, 35,
+        55, 12, 61, 73, 58, 27, 13, 37, 62, 63, 20, 39, 21, 34, 59, 14, 36, 52, 40, 38, 64, 75, 53, 65,
+        24, 15, 41, 16, 66, 72, 17, 42, 56, 25, 18, 19, 44, 43, 47, 57, 49, 45, 51, 46, 67, 74, 48, 69,
         50, 70, 68, 71,
     ),
     (
-        0, 1, 2, 3, 4, 5, 8, 6, 7, 14, 28, 29, 9, 15, 40, 41, 31, 22, 60, 10, 43, 16, 54, 30,
-        33, 45, 42, 23, 11, 17, 66, 35, 55, 12, 26, 32, 47, 73, 18, 44, 13, 63, 58, 27, 61, 37, 67, 19,
-        59, 69, 24, 20, 34, 49, 75, 46, 56, 39, 25, 21, 36, 52, 64, 62, 51, 48, 70, 57, 68, 53, 65, 38,
+        0, 1, 2, 3, 4, 5, 8, 6, 7, 14, 28, 9, 15, 40, 29, 22, 41, 10, 16, 30, 31, 60, 54, 43,
+        42, 23, 11, 33, 17, 45, 35, 12, 26, 32, 55, 47, 66, 18, 44, 13, 73, 27, 58, 37, 63, 19, 24, 61,
+        20, 59, 67, 49, 69, 39, 34, 25, 21, 56, 75, 46, 51, 52, 36, 64, 62, 57, 48, 53, 70, 68, 65, 38,
         74, 71, 50, 72,
     ),
     (
-        0, 1, 2, 3, 4, 5, 8, 6, 7, 20, 21, 22, 23, 9, 14, 52, 28, 29, 53, 10, 24, 40, 41, 54,
-        55, 11, 30, 31, 25, 72, 56, 12, 33, 60, 15, 73, 57, 32, 35, 13, 74, 37, 66, 26, 34, 43, 16, 61,
-        63, 27, 58, 36, 39, 42, 64, 59, 45, 62, 17, 75, 38, 65, 44, 47, 67, 69, 18, 46, 19, 49, 68, 51,
+        0, 1, 2, 3, 4, 5, 8, 6, 7, 22, 20, 23, 21, 9, 14, 28, 54, 10, 24, 40, 52, 29, 55, 11,
+        30, 25, 53, 41, 12, 15, 31, 73, 56, 32, 35, 13, 33, 60, 57, 72, 37, 26, 74, 16, 66, 27, 39, 34,
+        43, 42, 58, 61, 63, 59, 36, 64, 17, 45, 62, 44, 47, 75, 38, 65, 18, 19, 67, 69, 49, 46, 51, 68,
         48, 70, 50, 71,
     ),
     (
-        0, 1, 2, 3, 4, 5, 8, 9, 10, 11, 12, 13, 28, 29, 30, 31, 6, 7, 32, 33, 34, 35, 36, 37,
-        38, 39, 60, 63, 61, 64, 26, 20, 62, 65, 58, 52, 14, 15, 21, 40, 41, 53, 16, 42, 43, 72, 17, 45,
-        66, 18, 47, 44, 25, 19, 49, 57, 67, 24, 69, 22, 56, 46, 51, 54, 23, 74, 48, 70, 27, 55, 68, 59,
-        71, 50, 73, 75,
-    ),
-    (
-        0, 1, 2, 3, 4, 5, 8, 9, 10, 11, 12, 13, 28, 29, 30, 31, 6, 7, 32, 33, 34, 35, 36, 37,
-        38, 39, 60, 63, 61, 64, 22, 62, 65, 25, 54, 14, 57, 23, 15, 40, 41, 16, 43, 55, 42, 73, 17, 45,
-        66, 26, 18, 47, 58, 44, 19, 49, 67, 20, 69, 46, 21, 52, 51, 27, 24, 53, 48, 59, 70, 68, 50, 71,
-        56, 72, 75, 74,
-    ),
-    (
-        0, 1, 2, 3, 4, 5, 8, 6, 7, 22, 23, 20, 21, 9, 14, 54, 28, 29, 55, 10, 26, 40, 41, 52,
-        53, 11, 30, 31, 27, 73, 58, 12, 33, 60, 15, 72, 59, 32, 35, 13, 75, 37, 66, 24, 34, 43, 16, 61,
-        63, 25, 36, 39, 56, 42, 64, 57, 45, 62, 38, 65, 17, 74, 44, 18, 47, 67, 49, 46, 69, 19, 68, 70,
-        48, 51, 50, 71,
-    ),
-    (
-        0, 1, 2, 3, 4, 5, 8, 6, 7, 14, 28, 29, 9, 15, 40, 41, 31, 20, 60, 10, 43, 16, 52, 30,
-        33, 45, 42, 21, 11, 17, 66, 35, 53, 12, 32, 24, 72, 47, 18, 44, 13, 56, 63, 25, 61, 37, 67, 19,
-        57, 69, 26, 22, 34, 74, 49, 46, 58, 39, 36, 27, 23, 64, 54, 62, 51, 48, 70, 59, 68, 65, 55, 38,
-        71, 75, 50, 73,
-    ),
-    (
-        0, 1, 2, 3, 4, 5, 8, 6, 7, 9, 28, 29, 20, 30, 31, 10, 52, 60, 33, 21, 61, 11, 24, 53,
-        35, 32, 12, 34, 63, 56, 72, 25, 13, 62, 37, 22, 36, 57, 39, 23, 54, 38, 64, 14, 74, 65, 40, 55,
-        41, 66, 26, 73, 15, 58, 16, 17, 42, 43, 27, 18, 19, 44, 45, 59, 47, 46, 49, 67, 51, 75, 48, 69,
+        0, 1, 2, 3, 4, 5, 8, 9, 10, 11, 12, 13, 28, 6, 7, 30, 32, 29, 31, 35, 33, 37, 34, 39,
+        36, 38, 26, 20, 60, 63, 61, 64, 58, 14, 62, 65, 52, 15, 21, 40, 16, 42, 53, 17, 41, 18, 43, 72,
+        47, 44, 25, 19, 45, 49, 66, 24, 22, 57, 51, 23, 67, 56, 69, 54, 27, 46, 55, 74, 48, 70, 59, 68,
+        73, 71, 50, 75,
+    ),
+    (
+        0, 1, 2, 3, 4, 5, 8, 9, 10, 11, 12, 13, 28, 6, 7, 30, 32, 29, 31, 35, 33, 37, 34, 39,
+        36, 38, 60, 63, 22, 25, 61, 64, 54, 62, 65, 14, 23, 15, 57, 40, 16, 42, 41, 17, 55, 26, 43, 18,
+        47, 44, 73, 45, 66, 19, 58, 49, 20, 21, 67, 51, 27, 24, 52, 69, 46, 53, 59, 48, 68, 70, 56, 50,
+        71, 72, 75, 74,
+    ),
+    (
+        0, 1, 2, 3, 4, 5, 8, 6, 7, 20, 22, 21, 23, 9, 14, 28, 52, 10, 26, 30, 54, 29, 53, 11,
+        40, 27, 55, 31, 12, 15, 41, 72, 58, 32, 35, 33, 60, 59, 13, 73, 37, 24, 75, 16, 61, 25, 39, 34,
+        43, 42, 56, 63, 66, 36, 57, 64, 17, 45, 62, 18, 44, 47, 38, 65, 74, 49, 19, 67, 46, 69, 51, 48,
+        70, 68, 50, 71,
+    ),
+    (
+        0, 1, 2, 3, 4, 5, 8, 6, 7, 14, 28, 9, 15, 40, 29, 20, 41, 10, 16, 30, 31, 60, 52, 43,
+        42, 21, 11, 33, 17, 35, 12, 45, 24, 32, 53, 47, 66, 18, 44, 13, 72, 25, 56, 37, 63, 19, 26, 61,
+        22, 57, 67, 49, 69, 39, 34, 27, 23, 58, 74, 51, 46, 54, 36, 64, 62, 48, 59, 70, 55, 68, 65, 38,
+        75, 71, 50, 73,
+    ),
+    (
+        0, 1, 2, 3, 4, 5, 8, 6, 7, 28, 9, 20, 29, 10, 30, 52, 60, 31, 21, 11, 32, 24, 33, 35,
+        53, 12, 61, 72, 56, 25, 13, 37, 34, 63, 22, 39, 23, 62, 57, 14, 36, 54, 40, 38, 64, 74, 55, 65,
+        26, 15, 41, 66, 16, 73, 17, 42, 58, 27, 18, 19, 44, 43, 47, 59, 49, 45, 51, 46, 67, 75, 48, 69,
         50, 70, 68, 71,
     ),
     (
-        0, 1, 2, 3, 4, 5, 8, 6, 7, 28, 29, 9, 14, 60, 31, 20, 30, 10, 41, 52, 40, 33, 21, 61,
-        11, 35, 32, 53, 12, 66, 63, 24, 13, 72, 34, 37, 56, 15, 62, 39, 25, 36, 64, 16, 57, 38, 43, 26,
-        22, 74, 42, 65, 17, 58, 44, 45, 27, 54, 67, 18, 23, 47, 19, 46, 59, 49, 55, 68, 69, 75, 73, 48,
-        51, 70, 50, 71,
-    ),
-    (
-        0, 1, 2, 3, 4, 5, 8, 6, 7, 14, 28, 29, 9, 41, 15, 40, 20, 31, 24, 60, 10, 43, 52, 16,
-        30, 33, 56, 21, 42, 25, 45, 11, 17, 66, 53, 35, 32, 57, 18, 12, 47, 44, 72, 22, 63, 19, 23, 61,
-        74, 54, 13, 49, 67, 69, 55, 34, 26, 37, 73, 46, 58, 27, 51, 62, 70, 48, 59, 39, 36, 75, 64, 68,
+        0, 1, 2, 3, 4, 5, 8, 6, 7, 28, 9, 14, 29, 20, 30, 10, 60, 40, 31, 52, 21, 41, 11, 35,
+        32, 33, 12, 61, 53, 24, 13, 37, 66, 15, 63, 72, 56, 39, 25, 34, 62, 16, 57, 36, 26, 64, 22, 42,
+        38, 17, 43, 44, 74, 58, 65, 27, 18, 23, 47, 19, 54, 45, 49, 67, 59, 55, 46, 51, 68, 75, 69, 73,
+        48, 70, 50, 71,
+    ),
+    (
+        0, 1, 2, 3, 4, 5, 8, 6, 7, 14, 28, 9, 15, 40, 20, 29, 24, 41, 10, 16, 30, 31, 52, 60,
+        21, 42, 25, 43, 56, 11, 17, 33, 35, 53, 45, 32, 66, 18, 12, 47, 57, 44, 22, 23, 19, 72, 13, 49,
+        54, 63, 61, 74, 55, 26, 67, 37, 69, 34, 27, 51, 58, 73, 46, 62, 39, 59, 70, 48, 36, 75, 64, 68,
         71, 50, 65, 38,
     ),
     (
-        0, 1, 2, 3, 4, 5, 8, 6, 7, 9, 28, 29, 10, 30, 31, 11, 33, 60, 12, 32, 35, 37, 61, 13,
-        34, 63, 22, 14, 24, 36, 64, 54, 56, 39, 62, 23, 38, 41, 15, 27, 65, 55, 40, 43, 16, 59, 42, 73,
-        45, 66, 26, 17, 58, 44, 18, 47, 20, 75, 67, 52, 19, 49, 46, 21, 69, 25, 53, 68, 51, 48, 57, 50,
-        70, 72, 71, 74,
-    ),
-    (
-        0, 1, 2, 3, 4, 5, 8, 9, 10, 11, 12, 13, 28, 29, 30, 31, 6, 7, 20, 22, 21, 23, 32, 33,
-        52, 26, 54, 34, 35, 53, 27, 55, 36, 37, 14, 38, 39, 58, 72, 59, 15, 60, 63, 73, 75, 61, 64, 41,
-        62, 24, 40, 65, 16, 25, 42, 43, 56, 45, 66, 57, 17, 44, 74, 47, 67, 18, 69, 46, 49, 68, 19, 70,
-        48, 51, 50, 71,
+        0, 1, 2, 3, 4, 5, 8, 6, 7, 9, 28, 10, 30, 29, 11, 31, 12, 32, 35, 33, 60, 37, 13, 22,
+        24, 14, 61, 34, 63, 54, 39, 56, 36, 64, 23, 62, 15, 27, 40, 38, 41, 55, 16, 42, 65, 59, 43, 26,
+        17, 44, 73, 20, 18, 47, 45, 66, 58, 49, 19, 52, 21, 75, 67, 25, 69, 51, 46, 53, 70, 57, 68, 48,
+        50, 72, 71, 74,
+    ),
+    (
+        0, 1, 2, 3, 4, 5, 8, 9, 10, 11, 12, 13, 28, 6, 7, 30, 22, 20, 23, 21, 32, 29, 26, 31,
+        54, 35, 52, 33, 27, 55, 37, 34, 53, 14, 39, 36, 15, 58, 59, 73, 38, 60, 63, 72, 75, 61, 64, 24,
+        40, 41, 62, 16, 42, 25, 65, 56, 43, 17, 57, 44, 45, 66, 47, 18, 74, 49, 67, 69, 46, 19, 68, 70,
+        51, 48, 50, 71,
     ),
 )
 
@@ -183,7 +183,8 @@
                 peers.append((mod(x + dx, 4), y, zz, cc))
     team = [(mod(z_hi + d // 4, 4), mod(x + d % 4, 4)) for d in range(1, 16)]
     same_t = [(mod(z_hi + d // 4, 4), mod(y + d % 4, 4)) for d in range(1, 16)]
-    ends = [(zh, y, z_lo, xx, c) for zh, xx in team] + [(zh, yy, z_lo, x, c) for zh, yy in same_t]
+    ends = [(zh, y, z_lo, xx, c) for d, (zh, xx) in enumerate(team, 1) if d > 3 and d % 4]
+    ends += [(zh, yy, z_lo, x, c) for d, (zh, yy) in enumerate(same_t, 1) if d % 4 and d not in (1, 3)]
     for d in range(16):
         ends.append((d // 4, y, lax.rem(z_hi, 2), d % 4, z_hi // 2))
         ends.append((z_hi, d // 4, d % 2, y, (d // 2) % 2))
@@ -203,10 +204,17 @@
 
     chunks = [(0, 0), (1, 0), (2, 0), (0, 1), (1, 1), (2, 1)]
 
+    def lanes(j):
+        return pl.ds(pl.multiple_of(lax.rem(j, 4) * KB, KB), KB)
+
     def wslot(j, q):
         m, h = chunks[q]
-        n = KB // 2 if m < 2 else HID // 2
-        return (bwg, bwu, bwd)[m].at[j, pl.ds(h * n, n)]
+        if m == 2:
+            return bwd.at[j // 4, pl.ds(h * (HID // 2), HID // 2), lanes(j)]
+        return (bwg, bwu)[m].at[j, pl.ds(h * (KB // 2), KB // 2)]
+
+    def tslot(a, j):
+        return tok.at[a, j // 4, :, lanes(j)]
 
     def wsrc(q):
         m, h = chunks[q]
@@ -249,7 +257,7 @@
             elif kind == "ts":
                 a = arg[0]
                 j = z_lo * 8 + x * 2 + c
-                src, dst, sem = (src_n, src_g)[a], tok.at[a, j], r_tok.at[a, j]
+                src, dst, sem = (src_n, src_g)[a], tslot(a, j), r_tok.at[a, j]
                 if hop == 2 and i != c:
                     send(src, dst, sem, (x, y, z, i))
                 if hop == 2 and i == c and not drain:
@@ -286,7 +294,7 @@
                 u = us[n]
                 r = (r0 - u) % 8
                 j = u * 8 + x * 2 + cc
-                blk, sem = tok.at[a, j], r_tok.at[a, j]
+                blk, sem = tslot(a, j), r_tok.at[a, j]
                 await_(blk, sem)
                 if r in ((1, 2), (1,))[a]:
                     send(blk, blk, sem, (x, y, (z + 2) % 8, c))
@@ -297,7 +305,7 @@
             elif kind == "tx":
                 n, cc, a = arg
                 j = us[n] * 8 + (xm, xp)[a] * 2 + cc
-                blk, sem = tok.at[a, j], r_tok.at[a, j]
+                blk, sem = tslot(a, j), r_tok.at[a, j]
                 await_(blk, sem)
                 send(blk, blk, sem, ((xp, xm)[a], y, z, c))
             elif kind == "tw":
@@ -305,7 +313,7 @@
                 for a in (0, 1):
                     for xx in ((xp, xm)[a], mod(x + 2, 4)):
                         j = us[n] * 8 + xx * 2 + cc
-                        await_(tok.at[a, j], r_tok.at[a, j])
+                        await_(tslot(a, j), r_tok.at[a, j])
         return count[0]
 
     sent = {}
@@ -381,18 +389,15 @@
 
         pl.when(rest == 1)(wait_rest)
         js = pl.ds(zz * 4, 4)
-        n = jnp.concatenate([tok[0, zz * 4 + k] for k in range(4)], axis=1)
-        g = jnp.concatenate([tok[1, zz * 4 + k] for k in range(4)], axis=1)
-        down = jnp.concatenate([bwd[zz * 4 + k] for k in range(4)], axis=1)
-
         def add(acc, value):
             acc[...] = value if first else acc[...] + value
 
+        n = tok[0, zz]
         add(acc_g, jnp.dot(n, bwg[js].reshape(4 * KB, HID), preferred_element_type=F32))
         add(acc_u, jnp.dot(n, bwu[js].reshape(4 * KB, HID), preferred_element_type=F32))
         cols = pl.ds(pl.multiple_of(zz * (4 * KB), 4 * KB), 4 * KB)
         add(acc_l, lax.dot_general(n, pin[:, cols], (((1,), (1,)), ((), ())), preferred_element_type=F32))
-        add(acc_b, lax.dot_general(g, down, (((1,), (1,)), ((), ())), preferred_element_type=F32))
+        add(acc_b, lax.dot_general(tok[1, zz], bwd[zz], (((1,), (1,)), ((), ())), preferred_element_type=F32))
 
     product(0, True)
 
@@ -504,10 +509,10 @@
         in_specs=[vmem] * 2 + [any_] * 4 + [vmem] * 2 + [smem, vmem],
         out_specs=(vmem, vmem),
         scratch_shapes=[
-            pltpu.VMEM((2, NB, TOK, KB), BF16),
+            pltpu.VMEM((2, NB // 4, TOK, 4 * KB), BF16),
             pltpu.VMEM((NB, KB, HID), BF16),
             pltpu.VMEM((NB, KB, HID), BF16),
-            pltpu.VMEM((NB, HID, KB), BF16),
+            pltpu.VMEM((NB // 4, HID, 4 * KB), BF16),
             pltpu.VMEM((RANK, HID), BF16),
             pltpu.VMEM((TOK, HID), F32),
             pltpu.VMEM((TOK, HID), F32),

time: 161 us -> 158 us (0.981)
  Pallas kernels: 158 us -> 155 us
    pallas_call x1, Pallas kernels: 158 us -> 155 us  [gathered(): pl.pallas_call(gather_kernel, out_shape=(jax.ShapeDtypeStruct((RANK, RANK...]
where the time goes in v5:
time: 158 us
  Pallas kernels  155 us (98%)
  local copies, waits for them, and re-layouts  1.94 us (1%)
    pallas_call x1, Pallas kernels, gathered(): pl.pallas_call(gather_kernel, out_shape=(jax.ShapeDtypeStruct((RANK, RANK...  155 us

profile of v5, /device:TPU:32, one launch (start us, length us, event | category | flops | bytes accessed | tf_op | source)
XLA Modules:
  0.0 157.5 jit_solution(18446131850455646566)
XLA Ops:
  0.6 154.9 %shard_map.113 = (f32[64,64]{1,0:T(8,128)}, f32[1,256]{1,0:T(1,128)}) custom-call(bf16[512,256]{1,0:T(8,128)(2,1)} %bitcast.7, bf16[512,256]{1,0:T(8,128)(2,1)} %bitcast.8, bf16[256,896]{1,0:T(8,128)(2,1)} %wg.1, bf16[256,896]{1,0:T(8,128)(2,1)} %wu.1, bf16[896,256]{1,0:T(8,128)(2,1)} %wd.1, bf16[64,896]{1,0:T(8,128)(2,1)} %bitcast.9, ...), custom_call_target="tpu_custom_call" | custom-call | tf_op jit(solution)/shard_map/pallas_call | solution.py:503
  155.6 0.0 copy-start
  155.6 1.4 copy.14
  156.9 0.0 copy-done
  156.9 0.6 copy.15
Async XLA Ops:
  155.6 1.4 copy-start
